TPU v7x, 128 devices: a whole 4x4x4 slice. The times are simulated.
128 devices in a mesh: qrow: 16 (over z, y), kcol: 8 (over x, core).
Axes of the slice: x: 4, y: 4, z: 4, core: 2. Of those that a mesh axis runs over, the one named last changes fastest.
Arguments:
- features: bfloat16 [16384, 1024], P(('qrow', 'kcol')), may hold values from -24 to 24
- node_ids: int32 [16384], P(('qrow', 'kcol')), may hold values from 0 to 511
- token_embed: bfloat16 [512, 1024], replicated, may hold values from -3 to 3
- w_query: bfloat16 [1024, 1024], replicated, may hold values from -0.1875 to 0.1875
- w_key: bfloat16 [1024, 1024], replicated, may hold values from -0.1875 to 0.1875
- w_value: bfloat16 [1024, 1024], replicated, may hold values from -0.1875 to 0.1875
- w_out: bfloat16 [1024, 1024], replicated, may hold values from -0.1875 to 0.1875
- slopes: float32 [16], replicated, may hold values from 1 to 3
- chan_scale: float32 [64], replicated, may hold values from -6 to 6
- chan_shift: float32 [64], replicated, may hold values from -4 to 4
- edge_proj: bfloat16 [64, 32], replicated, may hold values from -0.75 to 0.75
- edge_value: bfloat16 [128, 8, 4, 128, 128], P('qrow', 'kcol'), may hold values from -4 to 240
- key_index: int32 [128, 8, 4], P('qrow', 'kcol'), may hold values from 0 to 15
- counts: int32 [128, 8], P('qrow', 'kcol'), may hold values from 0 to 4, as said below
- w_up: bfloat16 [1024, 4096], P(None, 'qrow'), may hold values from -0.1875 to 0.1875
- w_down: bfloat16 [4096, 1024], P('qrow'), may hold values from -0.09375 to 0.09375
Outputs:
- output: bfloat16 [16384, 1024], P(('qrow', 'kcol'))
Inputs may be any that keep to these rules, and one draw needn't show every extreme that they name: counts[g, c] is 1 or more in the column c = (g % 8), so every query node has a live tile.
All inputs are finite; a program needn't handle non-finite values.
Results may differ from a plain program's by a relative error of at most 0.013.
Values may be sent and summed in bfloat16 or wider, within the bound.
No kernel may reach another device: no remote copies, remote signals or barrier semaphores. Data moves between devices by JAX's collectives and lax.ppermute only.
A program may use at most 192 MiB of HBM per device.

v0:
```python
import jax
import jax.numpy as jnp
from jax import lax
from jax.sharding import PartitionSpec as P

NEG_FILL = -1e30


def joined(value, axis, join):
    pieces = jax.tree.map(lambda part: lax.all_gather(part, axis), value)
    head = jax.tree.map(lambda part: part[0], pieces)
    tail = jax.tree.map(lambda part: part[1:], pieces)
    so_far, _ = lax.scan(lambda so_far, section: (join(so_far, section), None), head, tail)
    return so_far


def layer_norm(values):
    average = jnp.mean(values, axis=-1, keepdims=True)
    centered = values - average
    spread = jnp.mean(centered * centered, axis=-1, keepdims=True)
    return centered * lax.rsqrt(spread + 1e-05)


def scale_heads(numer, factor):
    block_total, tile_rows, model_width = numer.shape
    head_count = factor.shape[1]
    shaped = numer.reshape(block_total, tile_rows, head_count, model_width // head_count)
    return (shaped * jnp.swapaxes(factor, 1, 2)[..., None]).reshape(
        block_total, tile_rows, model_width
    )


def tile_step(
    carried,
    queries,
    key_tiles,
    value_tiles,
    edge_tile,
    live_rows,
    slopes,
    chan_scale,
    chan_shift,
    edge_proj,
):
    run_max, run_sum, run_num = carried
    block_total, tile_rows, model_width = queries.shape
    head_count = slopes.shape[0]
    head_dim = model_width // head_count
    edge_f = edge_tile.astype(jnp.float32)
    channels = jax.nn.sigmoid(
        edge_f[:, None] * chan_scale[None, :, None, None] + chan_shift[None, :, None, None]
    ).astype(jnp.bfloat16)
    edge_terms = jnp.einsum(
        "aeij,eh->ahij", channels, edge_proj, preferred_element_type=jnp.float32
    )
    bias_part = edge_terms[:, :head_count]
    gate_part = jax.nn.sigmoid(edge_terms[:, head_count:])
    query_heads = queries.reshape(block_total, tile_rows, head_count, head_dim)
    key_heads = key_tiles.reshape(block_total, tile_rows, head_count, head_dim)
    value_heads = value_tiles.reshape(block_total, tile_rows, head_count, head_dim)
    scores = jnp.einsum(
        "aihd,ajhd->ahij", query_heads, key_heads, preferred_element_type=jnp.float32
    ) * head_dim ** (-0.5)
    scores = scores + bias_part + slopes[None, :, None, None] * edge_f[:, None]
    live_mask = live_rows[:, None, None, None]
    scores = jnp.where(live_mask, scores, NEG_FILL)
    new_max = jnp.maximum(run_max, jnp.max(scores, axis=-1))
    factor = jnp.exp(run_max - new_max)
    exp_scores = jnp.exp(scores - new_max[..., None]) * live_mask.astype(jnp.float32)
    run_sum = run_sum * factor + jnp.sum(exp_scores, axis=-1)
    gated = (exp_scores * gate_part).astype(jnp.bfloat16)
    contrib = jnp.einsum("ahij,ajhd->aihd", gated, value_heads, preferred_element_type=jnp.float32)
    run_num = scale_heads(run_num, factor) + contrib.reshape(block_total, tile_rows, model_width)
    return (new_max, run_sum, run_num)


def join_partials(first_part, second_part):
    max_one, sum_one, num_one = first_part
    max_two, sum_two, num_two = second_part
    joint_top = jnp.maximum(max_one, max_two)
    scale_one = jnp.exp(max_one - joint_top)
    scale_two = jnp.exp(max_two - joint_top)
    return (
        joint_top,
        sum_one * scale_one + sum_two * scale_two,
        scale_heads(num_one, scale_one) + scale_heads(num_two, scale_two),
    )


def local(
    features,
    node_ids,
    token_embed,
    w_query,
    w_key,
    w_value,
    w_out,
    slopes,
    chan_scale,
    chan_shift,
    edge_proj,
    edge_value,
    key_index,
    counts,
    w_up,
    w_down,
):
    node_dev, model_width = features.shape
    vocab_size = token_embed.shape[0]
    head_count = slopes.shape[0]
    tile_rows = edge_value.shape[-1]
    row_blocks = edge_value.shape[0]
    slot_count = edge_value.shape[2]
    blocks_own = node_dev // tile_rows
    one_hot = (
        node_ids[:, None] == lax.broadcasted_iota(jnp.int32, (node_dev, vocab_size), 1)
    ).astype(jnp.bfloat16)
    embedded = features.astype(jnp.float32) + jnp.dot(
        one_hot, token_embed, preferred_element_type=jnp.float32
    )
    normed = layer_norm(embedded).astype(jnp.bfloat16)
    query_own = jnp.dot(normed, w_query, preferred_element_type=jnp.float32).astype(jnp.bfloat16)
    key_own = jnp.dot(normed, w_key, preferred_element_type=jnp.float32).astype(jnp.bfloat16)
    value_own = jnp.dot(normed, w_value, preferred_element_type=jnp.float32).astype(jnp.bfloat16)
    queries = lax.all_gather(query_own, "kcol", axis=0, tiled=True).reshape(
        row_blocks, tile_rows, model_width
    )
    key_all, value_all = (
        lax.all_gather(key_own, "qrow", axis=0, tiled=True),
        lax.all_gather(value_own, "qrow", axis=0, tiled=True),
    )
    key_blocks = key_all.reshape(-1, tile_rows, model_width)
    value_blocks = value_all.reshape(-1, tile_rows, model_width)
    cell_edges = edge_value[:, 0]
    cell_index = key_index[:, 0]
    cell_counts = counts[:, 0]

    def visit_tile(slot_pos, carried):
        picked = lax.dynamic_index_in_dim(cell_index, slot_pos, 1, keepdims=False)
        edge_tile = lax.dynamic_index_in_dim(cell_edges, slot_pos, 1, keepdims=False)
        live_rows = cell_counts > slot_pos
        key_tiles = jnp.take(key_blocks, picked, axis=0)
        value_tiles = jnp.take(value_blocks, picked, axis=0)
        return tile_step(
            carried,
            queries,
            key_tiles,
            value_tiles,
            edge_tile,
            live_rows,
            slopes,
            chan_scale,
            chan_shift,
            edge_proj,
        )

    initial = (
        jnp.full((row_blocks, head_count, tile_rows), NEG_FILL, jnp.float32),
        jnp.zeros((row_blocks, head_count, tile_rows), jnp.float32),
        jnp.zeros((row_blocks, tile_rows, model_width), jnp.float32),
    )
    run_max, run_sum, run_num = lax.fori_loop(0, slot_count, visit_tile, initial)
    row_top, row_total, numerators = joined((run_max, run_sum, run_num), "kcol", join_partials)
    first_block = lax.axis_index("kcol") * blocks_own
    own_total = lax.dynamic_slice_in_dim(row_total, first_block, blocks_own, 0)
    own_num = lax.dynamic_slice_in_dim(numerators, first_block, blocks_own, 0)
    attended = (
        scale_heads(own_num, 1.0 / own_total).reshape(node_dev, model_width).astype(jnp.bfloat16)
    )
    residual = embedded + jnp.dot(attended, w_out, preferred_element_type=jnp.float32)
    normed_two = layer_norm(residual).astype(jnp.bfloat16)
    hidden = jax.nn.gelu(
        jnp.dot(
            lax.all_gather(normed_two, "qrow", axis=0, tiled=True),
            w_up,
            preferred_element_type=jnp.float32,
        ),
        approximate=False,
    ).astype(jnp.bfloat16)
    ffn_part = lax.psum_scatter(
        jnp.dot(hidden, w_down, preferred_element_type=jnp.float32).astype(jnp.bfloat16),
        "qrow",
        scatter_dimension=0,
        tiled=True,
    ).astype(jnp.float32)
    return (residual + ffn_part).astype(jnp.bfloat16)


def solution(mesh):
    placed = (
        P(("qrow", "kcol"), None),
        P(("qrow", "kcol")),
        P(),
        P(),
        P(),
        P(),
        P(),
        P(),
        P(),
        P(),
        P(),
        P("qrow", "kcol", None, None, None),
        P("qrow", "kcol", None),
        P("qrow", "kcol"),
        P(None, "qrow"),
        P("qrow", None),
    )
    return jax.shard_map(
        local, mesh=mesh, in_specs=placed, out_specs=P(("qrow", "kcol"), None), check_vma=False
    )
```

profile of v0, /device:TPU:1, one launch (start us, length us, event | category | flops | bytes accessed | tf_op | source)
XLA Modules:
  0.0 931.6 jit_solution(10296607309523637812)
XLA Ops:
  18.6 20.9 %all-gather.11.cloned.1.call-done = bf16[1024,1024]{1,0:T(8,128)(2,1)} async-done(((bf16[128,1024]{1,0:T(8,128)(2,1)}), bf16[1024,1024]{1,0:T(8,128)(2,1)}) %all-gather.11.cloned.1.call-update) | async-done | bytes 2097168 | tf_op jit(solution)/shard_map/all_gather | solution.py:125
  43.4 49.8 %all-gather.13.cloned.1.call-done = bf16[2048,1024]{1,0:T(8,128)(2,1)} async-done(((bf16[128,1024]{1,0:T(8,128)(2,1)}), bf16[2048,1024]{1,0:T(8,128)(2,1)}) %all-gather.13.cloned.1.call-update) | async-done | bytes 4194320 | tf_op jit(solution)/shard_map/all_gather | solution.py:130
  93.2 53.4 %all-gather.9.cloned.1.call-done = bf16[2048,1024]{1,0:T(8,128)(2,1)} async-done(((bf16[128,1024]{1,0:T(8,128)(2,1)}), bf16[2048,1024]{1,0:T(8,128)(2,1)}) %all-gather.9.cloned.1.call-update) | async-done | bytes 4194320 | tf_op jit(solution)/shard_map/all_gather | solution.py:129
  146.6 320.0 %while.33 = (s32[]{:T(128)}, f32[8,16,128]{2,1,0:T(8,128)S(1)}, f32[8,16,128]{2,1,0:T(8,128)S(1)}, f32[8,128,1024]{1,2,0:T(8,128)}, s32[8]{0:T(128)S(1)}, /*inde...) while((s32[]{:T(128)}, f32[8,16,128]{2,1,0:T(8,128)S(1)}, ...), condition=%wide.region_5.7_spmd.clone, body=%wide.region_2.6_spmd.clone.sunk | while | flops 1163101184 | bytes 224143984 | solution.py:162
  165.6 13.9 %fusion.139 = f32[8,128,128,32]{2,3,1,0:T(8,128)} fusion(f32[64]{0:T(128)S(1)} %get-tuple-element.641, f32[64]{0:T(128)S(1)} %get-tuple-element.640, f32[8,128,128]{2,1,0:T(8,128)S(1)} %copy.71, bf16[64,32]{0,1:T(8,128)(2,1)S(1)} %get-tuple-element.642), kind=kOutput, calls=%fused_computation.15.clone.1 | convolution fusion | flops 587202560 | bytes 17306112 | tf_op jit(solution)/shard_map/while/body/eval_jaxpr/aeij,eh->ahij/dot_general | solution.py:53
  179.6 17.4 %copy.72 = f32[8,128,128,32]{1,2,3,0:T(8,128)} copy(f32[8,128,128,32]{2,3,1,0:T(8,128)} %fusion.139) | data formatting | bytes 33554432 | tf_op jit(solution)/shard_map/while/body/eval_jaxpr/aeij,eh->ahij/dot_general | solution.py:53
  210.3 10.5 %fusion.144 = f32[8,16,64,128]{3,2,1,0:T(8,128)S(1)} fusion(bf16[8,128,16,64]{1,3,2,0:T(8,128)(2,1)} %bitcast.133, f32[8,32,128,128]{2,3,1,0:T(8,128)} %bitcast.128, f32[8,16,128,128]{2,3,1,0:T(8,128)} %get-tuple-element.595, f32[8]{0:T(128)S(1)} %get-tuple-element.596, f32[8,16,128]{2,1,0:T(8,128)S(1)} %get-tuple-element.632), kind=kOutput, calls=%fused_computation.33.clone.1 | convolution fusion | flops 283115520 | bytes 23134240 | tf_op jit(solution)/shard_map/while/body/eval_jaxpr/ahij,ajhd->aihd/dot_general | solution.py:72
  245.5 13.9 %fusion.139 = f32[8,128,128,32]{2,3,1,0:T(8,128)} fusion(f32[64]{0:T(128)S(1)} %get-tuple-element.641, f32[64]{0:T(128)S(1)} %get-tuple-element.640, f32[8,128,128]{2,1,0:T(8,128)S(1)} %copy.71, bf16[64,32]{0,1:T(8,128)(2,1)S(1)} %get-tuple-element.642), kind=kOutput, calls=%fused_computation.15.clone.1 | convolution fusion | flops 587202560 | bytes 17306112 | tf_op jit(solution)/shard_map/while/body/eval_jaxpr/aeij,eh->ahij/dot_general | solution.py:53
  259.5 17.4 %copy.72 = f32[8,128,128,32]{1,2,3,0:T(8,128)} copy(f32[8,128,128,32]{2,3,1,0:T(8,128)} %fusion.139) | data formatting | bytes 33554432 | tf_op jit(solution)/shard_map/while/body/eval_jaxpr/aeij,eh->ahij/dot_general | solution.py:53
  290.2 10.5 %fusion.144 = f32[8,16,64,128]{3,2,1,0:T(8,128)S(1)} fusion(bf16[8,128,16,64]{1,3,2,0:T(8,128)(2,1)} %bitcast.133, f32[8,32,128,128]{2,3,1,0:T(8,128)} %bitcast.128, f32[8,16,128,128]{2,3,1,0:T(8,128)} %get-tuple-element.595, f32[8]{0:T(128)S(1)} %get-tuple-element.596, f32[8,16,128]{2,1,0:T(8,128)S(1)} %get-tuple-element.632), kind=kOutput, calls=%fused_computation.33.clone.1 | convolution fusion | flops 283115520 | bytes 23134240 | tf_op jit(solution)/shard_map/while/body/eval_jaxpr/ahij,ajhd->aihd/dot_general | solution.py:72
  325.5 13.9 %fusion.139 = f32[8,128,128,32]{2,3,1,0:T(8,128)} fusion(f32[64]{0:T(128)S(1)} %get-tuple-element.641, f32[64]{0:T(128)S(1)} %get-tuple-element.640, f32[8,128,128]{2,1,0:T(8,128)S(1)} %copy.71, bf16[64,32]{0,1:T(8,128)(2,1)S(1)} %get-tuple-element.642), kind=kOutput, calls=%fused_computation.15.clone.1 | convolution fusion | flops 587202560 | bytes 17306112 | tf_op jit(solution)/shard_map/while/body/eval_jaxpr/aeij,eh->ahij/dot_general | solution.py:53
  339.4 17.4 %copy.72 = f32[8,128,128,32]{1,2,3,0:T(8,128)} copy(f32[8,128,128,32]{2,3,1,0:T(8,128)} %fusion.139) | data formatting | bytes 33554432 | tf_op jit(solution)/shard_map/while/body/eval_jaxpr/aeij,eh->ahij/dot_general | solution.py:53
  370.1 10.5 %fusion.144 = f32[8,16,64,128]{3,2,1,0:T(8,128)S(1)} fusion(bf16[8,128,16,64]{1,3,2,0:T(8,128)(2,1)} %bitcast.133, f32[8,32,128,128]{2,3,1,0:T(8,128)} %bitcast.128, f32[8,16,128,128]{2,3,1,0:T(8,128)} %get-tuple-element.595, f32[8]{0:T(128)S(1)} %get-tuple-element.596, f32[8,16,128]{2,1,0:T(8,128)S(1)} %get-tuple-element.632), kind=kOutput, calls=%fused_computation.33.clone.1 | convolution fusion | flops 283115520 | bytes 23134240 | tf_op jit(solution)/shard_map/while/body/eval_jaxpr/ahij,ajhd->aihd/dot_general | solution.py:72
  405.4 13.9 %fusion.139 = f32[8,128,128,32]{2,3,1,0:T(8,128)} fusion(f32[64]{0:T(128)S(1)} %get-tuple-element.641, f32[64]{0:T(128)S(1)} %get-tuple-element.640, f32[8,128,128]{2,1,0:T(8,128)S(1)} %copy.71, bf16[64,32]{0,1:T(8,128)(2,1)S(1)} %get-tuple-element.642), kind=kOutput, calls=%fused_computation.15.clone.1 | convolution fusion | flops 587202560 | bytes 17306112 | tf_op jit(solution)/shard_map/while/body/eval_jaxpr/aeij,eh->ahij/dot_general | solution.py:53
  419.3 17.4 %copy.72 = f32[8,128,128,32]{1,2,3,0:T(8,128)} copy(f32[8,128,128,32]{2,3,1,0:T(8,128)} %fusion.139) | data formatting | bytes 33554432 | tf_op jit(solution)/shard_map/while/body/eval_jaxpr/aeij,eh->ahij/dot_general | solution.py:53
  450.1 10.5 %fusion.144 = f32[8,16,64,128]{3,2,1,0:T(8,128)S(1)} fusion(bf16[8,128,16,64]{1,3,2,0:T(8,128)(2,1)} %bitcast.133, f32[8,32,128,128]{2,3,1,0:T(8,128)} %bitcast.128, f32[8,16,128,128]{2,3,1,0:T(8,128)} %get-tuple-element.595, f32[8]{0:T(128)S(1)} %get-tuple-element.596, f32[8,16,128]{2,1,0:T(8,128)S(1)} %get-tuple-element.632), kind=kOutput, calls=%fused_computation.33.clone.1 | convolution fusion | flops 283115520 | bytes 23134240 | tf_op jit(solution)/shard_map/while/body/eval_jaxpr/ahij,ajhd->aihd/dot_general | solution.py:72
  472.1 13.9 %all-gather = f32[64,16,128]{2,1,0:T(8,128)S(1)} all-gather(f32[8,16,128]{2,1,0:T(8,128)S(1)} %get-tuple-element.275), channel_id=2, replica_groups=mesh['qrow'=16,'kcol'=8] {'kcol'}, dimensions={0}, use_global_device_ids=true | all-gather | bytes 589824 | tf_op jit(solution)/shard_map/all_gather | solution.py:10
  486.9 14.2 %all-gather.1 = f32[64,16,128]{2,1,0:T(8,128)S(1)} all-gather(f32[8,16,128]{2,1,0:T(8,128)S(1)} %get-tuple-element.276), channel_id=3, replica_groups=mesh['qrow'=16,'kcol'=8] {'kcol'}, dimensions={0}, use_global_device_ids=true | all-gather | bytes 589824 | tf_op jit(solution)/shard_map/all_gather | solution.py:10
  502.0 127.8 %all-gather.17.cloned.1.call-done = f32[64,128,1024]{2,1,0:T(8,128)} async-done(((f32[8,128,1024]{2,1,0:T(8,128)}), f32[64,128,1024]{2,1,0:T(8,128)}) %all-gather.17.cloned.1.call-update) | async-done | bytes 33554448 | tf_op jit(solution)/shard_map/all_gather | solution.py:10
  639.9 22.0 %slice.57 = f32[56,128,1024]{2,1,0:T(8,128)} slice(f32[64,128,1024]{2,1,0:T(8,128)} %all-gather.17.cloned.1.call-done), slice={[8:64], [0:128], [0:1024]} | slice | bytes 58720256 | tf_op jit(solution)/shard_map/slice | solution.py:12
  662.0 118.6 %while.32 = (s32[]{:T(128)}, f32[8,16,128]{2,1,0:T(8,128)S(1)}, f32[8,16,128]{2,1,0:T(8,128)S(1)}, f32[8,128,1024]{1,2,0:T(8,128)}, f32[7,8,16,128]{3,2,1,0:T(8,...) while((s32[]{:T(128)}, f32[8,16,128]{2,1,0:T(8,128)S(1)}, ...), condition=%wide.region_7.9_spmd, body=%wide.region_6.8_spmd.sunk | while | flops 3260418 | bytes 30343264 | solution.py:13
  783.3 52.1 %all-gather.15.cloned.1.call-done = bf16[2048,1024]{1,0:T(8,128)(2,1)} async-done(((bf16[128,1024]{1,0:T(8,128)(2,1)}), bf16[2048,1024]{1,0:T(8,128)(2,1)}) %all-gather.15.cloned.1.call-update) | async-done | bytes 4194320 | tf_op jit(solution)/shard_map/all_gather | solution.py:174
  835.4 11.6 %convolution_convert_fusion = bf16[2048,1024]{1,0:T(8,128)(2,1)} fusion(bf16[256,1024]{1,0:T(8,128)(2,1)} %param.37, bf16[2048,1024]{1,0:T(8,128)(2,1)} %all-gather.15.cloned.1.call-done, bf16[1024,256]{1,0:T(8,128)(2,1)} %param.36), kind=kOutput, calls=%fused_computation.50 | convolution fusion | flops 2183659520 | bytes 9437184 | tf_op jit(solution)/shard_map/dot_general | solution.py:181
  847.1 75.9 %reduce-scatter.2.cloned.1.call-done = bf16[128,1024]{1,0:T(8,128)(2,1)} async-done(((bf16[2048,1024]{1,0:T(8,128)(2,1)}), bf16[128,1024]{1,0:T(8,128)(2,1)}) %reduce-scatter.2.cloned.1.call-update) | async-done | bytes 262160 | tf_op jit(solution)/shard_map/reduce_scatter | solution.py:180
  (202 shorter events, 308.2 us)
Async XLA Ops:
  6.5 775.1 %copy-start = (bf16[1024,1024]{1,0:T(8,128)(2,1)S(1)}, bf16[1024,1024]{1,0:T(8,128)(2,1)}, u32[]{:S(2)}) copy-start(bf16[1024,1024]{1,0:T(8,128)(2,1)} %param.28) | copy-start | bytes 6291460
  6.5 32.9 %all-gather.11.cloned.1.call-start = ((), (), s32[]{:S(2)}) async-start(), calls=%async_computation.2 | async-start | bytes 2359296 | tf_op jit(solution)/shard_map/all_gather | solution.py:125
  6.5 2.8 copy-start.9
  10.5 82.6 %all-gather.13.cloned.1.call-start = ((), (), s32[]{:S(2)}) async-start(), calls=%async_computation.3 | async-start | bytes 4456448 | tf_op jit(solution)/shard_map/all_gather | solution.py:130
  13.4 133.2 %all-gather.9.cloned.1.call-start = ((), (), s32[]{:S(2)}) async-start(), calls=%async_computation.1 | async-start | bytes 4456448 | tf_op jit(solution)/shard_map/all_gather | solution.py:129
  16.2 613.6 %all-gather.17.cloned.1.call-start = ((), (), s32[]{:S(2)}) async-start(), calls=%async_computation.6 | async-start | bytes 37748736 | tf_op jit(solution)/shard_map/all_gather | solution.py:10
  18.5 128.1 %copy-start.10 = (f32[16]{0:T(128)S(1)}, f32[16]{0:T(128)}, u32[]{:S(2)}) copy-start(f32[16]{0:T(128)} %param.29) | copy-start | bytes 196
  18.5 128.1 %copy-start.11 = (s32[8,1]{0,1:T(1,128)S(1)}, s32[8,1]{0,1:T(1,128)}, u32[]{:S(2)}) copy-start(s32[8,1]{0,1:T(1,128)} %param.35) | copy-start | bytes 100
  18.5 128.1 %copy-start.12 = (bf16[64,32]{0,1:T(8,128)(2,1)S(1)}, bf16[64,32]{0,1:T(8,128)(2,1)}, u32[]{:S(2)}) copy-start(bf16[64,32]{0,1:T(8,128)(2,1)} %param.32) | copy-start | bytes 12292
  18.5 128.1 %copy-start.13 = (f32[64]{0:T(128)S(1)}, f32[64]{0:T(128)}, u32[]{:S(2)}) copy-start(f32[64]{0:T(128)} %param.30) | copy-start | bytes 772
  18.6 128.1 %copy-start.14 = (f32[64]{0:T(128)S(1)}, f32[64]{0:T(128)}, u32[]{:S(2)}) copy-start(f32[64]{0:T(128)} %param.31) | copy-start | bytes 772
  210.3 10.5 %copy-start.3 = (f32[8,128,1024]{1,2,0:T(8,128)S(1)}, f32[8,128,1024]{1,2,0:T(8,128)}, u32[]{:S(2)}) copy-start(f32[8,128,1024]{1,2,0:T(8,128)} %get-tuple-element.618) | copy-start | bytes 12582916 | tf_op jit(solution)/shard_map/while
  220.8 3.4 copy-start.1
  290.2 10.5 %copy-start.3 = (f32[8,128,1024]{1,2,0:T(8,128)S(1)}, f32[8,128,1024]{1,2,0:T(8,128)}, u32[]{:S(2)}) copy-start(f32[8,128,1024]{1,2,0:T(8,128)} %get-tuple-element.618) | copy-start | bytes 12582916 | tf_op jit(solution)/shard_map/while
  300.7 3.4 copy-start.1
  370.1 10.5 %copy-start.3 = (f32[8,128,1024]{1,2,0:T(8,128)S(1)}, f32[8,128,1024]{1,2,0:T(8,128)}, u32[]{:S(2)}) copy-start(f32[8,128,1024]{1,2,0:T(8,128)} %get-tuple-element.618) | copy-start | bytes 12582916 | tf_op jit(solution)/shard_map/while
  380.6 3.4 copy-start.1
  450.0 10.5 %copy-start.3 = (f32[8,128,1024]{1,2,0:T(8,128)S(1)}, f32[8,128,1024]{1,2,0:T(8,128)}, u32[]{:S(2)}) copy-start(f32[8,128,1024]{1,2,0:T(8,128)} %get-tuple-element.618) | copy-start | bytes 12582916 | tf_op jit(solution)/shard_map/while
  460.5 3.4 copy-start.1
  472.1 363.4 %all-gather.15.cloned.1.call-start = ((), (), s32[]{:S(2)}) async-start(), calls=%async_computation.4 | async-start | bytes 4456448 | tf_op jit(solution)/shard_map/all_gather | solution.py:174
  639.9 22.0 %slice-start = ((f32[64,16,128]{2,1,0:T(8,128)}), f32[8,16,128]{2,1,0:T(8,128)S(1)}, s32[]{:S(2)}) async-start(f32[64,16,128]{2,1,0:T(8,128)} %copy-done.7), calls=%async_computation.7 | async-start | bytes 131072 | tf_op jit(solution)/shard_map/slice | solution.py:11
  639.9 22.0 %slice-start.1 = ((f32[64,16,128]{2,1,0:T(8,128)}), f32[8,16,128]{2,1,0:T(8,128)S(1)}, s32[]{:S(2)}) async-start(f32[64,16,128]{2,1,0:T(8,128)} %copy-done.8), calls=%async_computation.8 | async-start | bytes 131072 | tf_op jit(solution)/shard_map/slice | solution.py:11
  662.0 119.7 %copy-start.6 = (f32[128,1024]{1,0:T(8,128)S(1)}, f32[128,1024]{1,0:T(8,128)}, u32[]{:S(2)}) copy-start(f32[128,1024]{1,0:T(8,128)} %copy-done.5) | copy-start | bytes 1572868
  783.3 139.8 %reduce-scatter.2.cloned.1.call-start = ((), (), s32[]{:S(2)}) async-start(), calls=%async_computation.5 | async-start | bytes 4456448 | tf_op jit(solution)/shard_map/reduce_scatter | solution.py:180
  (11 other events, 21.8 us)
Sparse Core Ops, SparseCore 0:
  10.6 28.7 all-gather.10
  41.6 51.5 all-gather.12
  95.3 51.2 all-gather.8
  472.2 157.5 all-gather.16
  783.4 51.9 all-gather.14
  847.2 75.7 reduce-scatter.1
where the time goes:
time: 936 us; the launch traced here: 932 us
  waiting for transfers between devices  380 us (41%)
  local copies, waits for them, and re-layouts  270 us (29%)
  matrix products  146 us (16%)
  other arithmetic  92.5 us (10%)
  blocking collectives  28.1 us (3%)
  between operations  13.6 us (1%)
    all_gather x1, waiting for transfers between devices, joined(): pieces = jax.tree.map(lambda part: lax.all_gather(part, axis), value)  128 us
    reduce_scatter x1, waiting for transfers between devices, local(): lax.psum_scatter(jnp.dot(hidden, w_down, preferred_element_type=jnp.float...  75.9 us
    dynamic_slice x14, local copies, waits for them, and re-layouts, joined(): lax.scan(lambda so_far, section: (join(so_far, section), None), head, tail)  70.7 us
    dot_general x4, local copies, waits for them, and re-layouts, tile_step(): jnp.einsum('aeij,eh->ahij', channels, edge_proj, preferred_element_type=j...  69.6 us
    dot_general x4, matrix products, tile_step(): jnp.einsum('aeij,eh->ahij', channels, edge_proj, preferred_element_type=j...  55.8 us
    all_gather x1, waiting for transfers between devices, local(): lax.all_gather(key_own, 'qrow', axis=0, tiled=True)  53.4 us
    all_gather x1, waiting for transfers between devices, local(): lax.all_gather(normed_two, 'qrow', axis=0, tiled=True)  52.1 us
    all_gather x1, waiting for transfers between devices, local(): lax.all_gather(value_own, 'qrow', axis=0, tiled=True)  49.8 us
  transfers between devices with their start and end apart: 6, of which 6 were waited for; matrix products, arithmetic and copies ran while one was open for 1% of the time, Pallas kernels for 0%

commit v1 on v0

v1 whole, which is shorter than its diff:
```python
import jax
import jax.numpy as jnp
from jax import lax
from jax.experimental import pallas as pl
from jax.experimental.pallas import tpu as pltpu
from jax.sharding import PartitionSpec as P

NEG_FILL = -1e30
VMEM_BYTES = 56 * 1024 * 1024


def layer_norm(values):
    average = jnp.mean(values, axis=-1, keepdims=True)
    centered = values - average
    spread = jnp.mean(centered * centered, axis=-1, keepdims=True)
    return centered * lax.rsqrt(spread + 1e-05)


def edge_kernel(
    tile_of,
    slot_of,
    live_of,
    slopes,
    offsets,
    edge_ref,
    mix_ref,
    scale_ref,
    shift_ref,
    base_ref,
    gate_ref,
    edge_t,
    chans,
):
    step = pl.program_id(0)
    heads = base_ref.shape[1]
    rows, lanes = edge_t.shape
    channel_count = scale_ref.shape[0]

    @pl.when(live_of[step] > 0)
    def _():
        edge_t[...] = edge_ref[0].astype(jnp.float32).T
        scale = scale_ref[...]
        shift = shift_ref[...]
        for part in range(rows // 16):
            slot = part % 2
            for half in range(2):
                for within in range(8):
                    row = part * 16 + half * 8 + within
                    line = jnp.broadcast_to(edge_t[row : row + 1, :], scale.shape)
                    pre = (line * scale + shift).astype(jnp.bfloat16)
                    chans[
                        slot,
                        within * channel_count : (within + 1) * channel_count,
                        half * lanes : (half + 1) * lanes,
                    ] = jnp.tanh(pre)
            terms = jnp.dot(mix_ref[...], chans[slot], preferred_element_type=jnp.float32)
            low = edge_t[part * 16 : part * 16 + 8, :]
            high = edge_t[part * 16 + 8 : part * 16 + 16, :]
            for head in range(heads):
                block = terms[head * 8 : head * 8 + 8]
                base_ref[0, head, part * 16 : part * 16 + 8, :] = block[:, :lanes] + (
                    low * slopes[head] + offsets[head]
                )
                base_ref[0, head, part * 16 + 8 : part * 16 + 16, :] = block[:, lanes:] + (
                    high * slopes[head] + offsets[head]
                )
                gate_block = terms[(heads + head) * 8 : (heads + head) * 8 + 8]
                both = jnp.concatenate([gate_block[:, :lanes], gate_block[:, lanes:]], axis=0)
                gate_ref[0, head, part * 16 : part * 16 + 16, :] = (
                    0.5 + 0.5 * jnp.tanh(both + offsets[heads + head])
                ).astype(jnp.bfloat16)


def edge_stage(tile_of, slot_of, live_of, slopes, offsets, edges, mix, scale, shift):
    tiles, rows, lanes = edges.shape
    heads = slopes.shape[0]
    grid_spec = pltpu.PrefetchScalarGridSpec(
        num_scalar_prefetch=5,
        grid=(tiles,),
        in_specs=[
            pl.BlockSpec((1, rows, lanes), lambda s, tile, *_: (tile[s], 0, 0)),
            pl.BlockSpec(mix.shape, lambda s, *_: (0, 0)),
            pl.BlockSpec(scale.shape, lambda s, *_: (0, 0)),
            pl.BlockSpec(shift.shape, lambda s, *_: (0, 0)),
        ],
        out_specs=[
            pl.BlockSpec((1, heads, rows, lanes), lambda s, tile, slot, *_: (slot[s], 0, 0, 0)),
            pl.BlockSpec((1, heads, rows, lanes), lambda s, tile, slot, *_: (slot[s], 0, 0, 0)),
        ],
        scratch_shapes=[
            pltpu.VMEM((rows, lanes), jnp.float32),
            pltpu.VMEM((2, mix.shape[1], 2 * lanes), jnp.bfloat16),
        ],
    )
    return pl.pallas_call(
        edge_kernel,
        grid_spec=grid_spec,
        out_shape=[
            jax.ShapeDtypeStruct((tiles, heads, rows, lanes), jnp.float32),
            jax.ShapeDtypeStruct((tiles, heads, rows, lanes), jnp.bfloat16),
        ],
        compiler_params=pltpu.CompilerParams(vmem_limit_bytes=VMEM_BYTES),
        cost_estimate=pl.CostEstimate(
            flops=tiles * 2 * rows * lanes * 64 * 256,
            bytes_accessed=tiles * rows * lanes * heads * 6,
            transcendentals=tiles * rows * lanes * 80,
        ),
        name="edge_terms",
    )(tile_of, slot_of, live_of, slopes, offsets, edges, mix, scale, shift)


def attend_kernel(
    slot_of,
    block_of,
    key_of,
    live_of,
    first_of,
    last_of,
    base_ref,
    gate_ref,
    key_ref,
    value_ref,
    query_ref,
    num_ref,
    stat_ref,
    query_pairs,
    acc,
    tops,
    totals,
):
    step = pl.program_id(0)
    heads = base_ref.shape[1]
    rows = base_ref.shape[2]
    lanes = base_ref.shape[3]
    head_dim = acc.shape[0] // heads

    @pl.when(first_of[step] > 0)
    def _():
        block = block_of[step]
        acc[...] = jnp.zeros_like(acc)
        tops[...] = jnp.full_like(tops, NEG_FILL)
        totals[...] = jnp.zeros_like(totals)
        blank = jnp.zeros((head_dim, lanes), jnp.bfloat16)
        for pair in range(heads // 2):
            upper = query_ref[block, pair * 2 * head_dim : (pair * 2 + 1) * head_dim, :]
            lower = query_ref[block, (pair * 2 + 1) * head_dim : (pair * 2 + 2) * head_dim, :]
            query_pairs[pair, :head_dim, :lanes] = upper
            query_pairs[pair, :head_dim, lanes:] = blank
            query_pairs[pair, head_dim:, :lanes] = blank
            query_pairs[pair, head_dim:, lanes:] = lower

    @pl.when(live_of[step] > 0)
    def _():
        key_block = key_of[step]
        for pair in range(heads // 2):
            width = 2 * head_dim
            keys = key_ref[key_block, :, pair * width : (pair + 1) * width]
            both = jnp.dot(keys, query_pairs[pair], preferred_element_type=jnp.float32)
            for side in range(2):
                head = pair * 2 + side
                span = slice(head * head_dim, (head + 1) * head_dim)
                scores = both[:, side * lanes : (side + 1) * lanes] + base_ref[0, head]
                old_top = tops[head : head + 1, :]
                new_top = jnp.maximum(old_top, jnp.max(scores, axis=0, keepdims=True))
                factor = jnp.exp(old_top - new_top)
                weights = jnp.exp(scores - new_top)
                totals[head : head + 1, :] = totals[head : head + 1, :] * factor + jnp.sum(
                    weights, axis=0, keepdims=True
                )
                tops[head : head + 1, :] = new_top
                gated = (weights * gate_ref[0, head].astype(jnp.float32)).astype(jnp.bfloat16)
                part = jnp.dot(
                    value_ref[key_block, span, :], gated, preferred_element_type=jnp.float32
                )
                acc[span, :] = acc[span, :] * factor + part

    @pl.when(last_of[step] > 0)
    def _():
        for head in range(heads):
            span = slice(head * head_dim, (head + 1) * head_dim)
            total = totals[head : head + 1, :]
            inverse = jnp.where(total > 0.0, 1.0 / jnp.where(total > 0.0, total, 1.0), 0.0)
            num_ref[0, span, :] = (acc[span, :] * inverse).astype(num_ref.dtype)
        stat_ref[0, :heads, :] = tops[...]
        stat_ref[0, heads:, :] = totals[...]


def attend_stage(lists, base, gate, keys, values, queries):
    block_total, width, lanes = queries.shape
    tiles, heads, rows, _ = base.shape
    whole = lambda array: pl.BlockSpec(
        array.shape, lambda s, *_: (0,) * array.ndim, pipeline_mode=pl.Buffered(1)
    )
    grid_spec = pltpu.PrefetchScalarGridSpec(
        num_scalar_prefetch=6,
        grid=(tiles,),
        in_specs=[
            pl.BlockSpec((1, heads, rows, lanes), lambda s, slot, *_: (slot[s], 0, 0, 0)),
            pl.BlockSpec((1, heads, rows, lanes), lambda s, slot, *_: (slot[s], 0, 0, 0)),
            whole(keys),
            whole(values),
            whole(queries),
        ],
        out_specs=[
            pl.BlockSpec((1, width, lanes), lambda s, slot, block, *_: (block[s], 0, 0)),
            pl.BlockSpec((1, 2 * heads, lanes), lambda s, slot, block, *_: (block[s], 0, 0)),
        ],
        scratch_shapes=[
            pltpu.VMEM((heads // 2, 2 * width // heads, 2 * lanes), jnp.bfloat16),
            pltpu.VMEM((width, lanes), jnp.float32),
            pltpu.VMEM((heads, lanes), jnp.float32),
            pltpu.VMEM((heads, lanes), jnp.float32),
        ],
    )
    return pl.pallas_call(
        attend_kernel,
        grid_spec=grid_spec,
        out_shape=[
            jax.ShapeDtypeStruct((block_total, width, lanes), jnp.bfloat16),
            jax.ShapeDtypeStruct((block_total, 2 * heads, lanes), jnp.float32),
        ],
        compiler_params=pltpu.CompilerParams(vmem_limit_bytes=VMEM_BYTES),
        cost_estimate=pl.CostEstimate(
            flops=tiles * 4 * rows * lanes * width,
            bytes_accessed=tiles * rows * lanes * heads * 6,
            transcendentals=tiles * rows * lanes * heads,
        ),
        name="attend",
    )(*lists, base, gate, keys, values, queries)


def step_lists(cell_counts, cell_index):
    block_total, slot_count = cell_index.shape
    total = block_total * slot_count
    slots = jnp.arange(slot_count, dtype=jnp.int32)[None, :]
    visits = jnp.maximum(cell_counts, 1)[:, None]
    used = (slots < visits).reshape(total)
    order = jnp.arange(total, dtype=jnp.int32)
    place = jnp.sum((used[None, :] & (order[None, :] < order[:, None])).astype(jnp.int32), axis=1)
    steps = jnp.sum(used.astype(jnp.int32))
    slot_of = jnp.minimum(order, steps - 1)
    chosen = used[None, :] & (place[None, :] == slot_of[:, None])
    fresh = (order < steps).astype(jnp.int32)
    pick = lambda values: jnp.sum(
        jnp.where(chosen, values.reshape(1, total).astype(jnp.int32), 0), axis=1
    )
    blocks = jnp.broadcast_to(
        jnp.arange(block_total, dtype=jnp.int32)[:, None], (block_total, slot_count)
    )
    tile_of = pick(order)
    block_of = pick(blocks)
    key_of = pick(cell_index)
    live_of = pick(slots < cell_counts[:, None]) * fresh
    first_of = pick(jnp.broadcast_to(slots == 0, (block_total, slot_count))) * fresh
    last_of = pick(slots == visits - 1) * fresh
    return tile_of, slot_of, block_of, key_of, live_of, first_of, last_of


def mix_matrix(edge_proj, heads):
    channel_count, outs = edge_proj.shape
    factors = jnp.where(jnp.arange(outs) < heads, 0.5, 0.25).astype(jnp.bfloat16)
    scaled = (edge_proj * factors[None, :]).T
    eye = jnp.eye(8, dtype=jnp.bfloat16)
    mixed = scaled[:, None, None, :] * eye[None, :, :, None]
    offsets = jnp.sum(scaled.astype(jnp.float32), axis=1)
    return mixed.reshape(outs * 8, 8 * channel_count), offsets


def local(
    features,
    node_ids,
    token_embed,
    w_query,
    w_key,
    w_value,
    w_out,
    slopes,
    chan_scale,
    chan_shift,
    edge_proj,
    edge_value,
    key_index,
    counts,
    w_up,
    w_down,
):
    node_dev, width = features.shape
    vocab_size = token_embed.shape[0]
    heads = slopes.shape[0]
    head_dim = width // heads
    rows = edge_value.shape[-1]
    one_hot = (
        node_ids[:, None] == lax.broadcasted_iota(jnp.int32, (node_dev, vocab_size), 1)
    ).astype(jnp.bfloat16)
    embedded = features.astype(jnp.float32) + jnp.dot(
        one_hot, token_embed, preferred_element_type=jnp.float32
    )
    normed = layer_norm(embedded).astype(jnp.bfloat16)
    row_nodes = lax.all_gather(normed, "kcol", axis=0)
    column_nodes = lax.all_gather(normed, "qrow", axis=0)
    up_all = lax.all_gather(w_up, "qrow", axis=0)
    down_all = lax.all_gather(w_down, "qrow", axis=0)

    tile_of, slot_of, block_of, key_of, live_of, first_of, last_of = step_lists(
        counts[:, 0], key_index[:, 0]
    )
    mix, offsets = mix_matrix(edge_proj, heads)
    spread = lambda vector: jnp.broadcast_to((0.5 * vector)[:, None], (vector.shape[0], rows))
    base, gate = edge_stage(
        tile_of,
        slot_of,
        live_of,
        slopes,
        offsets,
        edge_value.reshape(-1, rows, rows),
        mix,
        spread(chan_scale),
        spread(chan_shift),
    )
    queries = (
        jnp.einsum("kd,gnk->gdn", w_query, row_nodes, preferred_element_type=jnp.float32).astype(
            jnp.bfloat16
        )
        * jnp.bfloat16(head_dim ** (-0.5))
    )
    keys = jnp.einsum(
        "gnk,kd->gnd", column_nodes, w_key, preferred_element_type=jnp.float32
    ).astype(jnp.bfloat16)
    values = jnp.einsum(
        "kd,gnk->gdn", w_value, column_nodes, preferred_element_type=jnp.float32
    ).astype(jnp.bfloat16)
    partial, stats = attend_stage(
        (slot_of, block_of, key_of, live_of, first_of, last_of), base, gate, keys, values, queries
    )
    partial = lax.all_to_all(partial, "kcol", 0, 0, tiled=True)
    stats = lax.all_to_all(stats, "kcol", 0, 0, tiled=True)
    tops, totals = stats[:, :heads], stats[:, heads:]
    shares = totals * jnp.exp(tops - jnp.max(tops, axis=0, keepdims=True))
    shares = shares / jnp.sum(shares, axis=0, keepdims=True)
    attended = jnp.sum(
        partial.astype(jnp.float32).reshape(-1, heads, head_dim, rows) * shares[:, :, None, :],
        axis=0,
    )
    attended = attended.reshape(width, rows).T.astype(jnp.bfloat16)
    residual = embedded + jnp.dot(attended, w_out, preferred_element_type=jnp.float32)
    normed_two = layer_norm(residual).astype(jnp.bfloat16)
    hidden = jax.nn.gelu(
        jnp.einsum("nk,skf->snf", normed_two, up_all, preferred_element_type=jnp.float32),
        approximate=False,
    ).astype(jnp.bfloat16)
    ffn = jnp.einsum("snf,sfd->nd", hidden, down_all, preferred_element_type=jnp.float32)
    return (residual + ffn).astype(jnp.bfloat16)


def solution(mesh):
    placed = (
        P(("qrow", "kcol"), None),
        P(("qrow", "kcol")),
        P(),
        P(),
        P(),
        P(),
        P(),
        P(),
        P(),
        P(),
        P(),
        P("qrow", "kcol", None, None, None),
        P("qrow", "kcol", None),
        P("qrow", "kcol"),
        P(None, "qrow"),
        P("qrow", None),
    )
    return jax.shard_map(
        local, mesh=mesh, in_specs=placed, out_specs=P(("qrow", "kcol"), None), check_vma=False
    )
```

time: 936 us -> 256 us (0.27)
  local copies, waits for them, and re-layouts: 270 us -> 4.18 us
  waiting for transfers between devices: 380 us -> 116 us
  matrix products: 146 us -> 33.7 us
  other arithmetic: 92.5 us -> 7.95 us
  Pallas kernels: 0 us -> 62.4 us
  blocking collectives: 28.1 us -> 12.4 us
    all_gather x5 -> x4, waiting for transfers between devices: 304 us -> 88 us  [the longest x1 56.2 us: local(): down_all = lax.all_gather(w_down, 'qrow', axis=0)]
    dot_general x16 -> x4, matrix products: 144 us -> 31.3 us  [the longest x1 11.4 us: local(): jnp.einsum('snf,sfd->nd', hidden, down_all, preferred_element_type=jnp.fl...]
    reduce_scatter x1 -> x0, waiting for transfers between devices: 75.9 us -> none  [local(): lax.psum_scatter(jnp.dot(hidden, w_down, preferred_element_type=jnp.float...]
    dynamic_slice x14 -> x0, local copies, waits for them, and re-layouts: 70.7 us -> none  [joined(): lax.scan(lambda so_far, section: (join(so_far, section), None), head, tail)]
    dot_general x4 -> x0, local copies, waits for them, and re-layouts: 69.6 us -> none  [tile_step(): jnp.einsum('aeij,eh->ahij', channels, edge_proj, preferred_element_type=j...]
    pallas_call x0 -> x2, Pallas kernels: none -> 62.4 us  [the longest x1 32.9 us: edge_stage(): pl.pallas_call(edge_kernel, grid_spec=grid_spec, out_shape=[jax.ShapeDtyp...]
    add x15 -> x0, other arithmetic: 46.6 us -> none  [the longest x7 41.3 us: join_partials(): scale_heads(num_one, scale_one) + scale_heads(num_two, scale_two)]
    gather x8 -> x0, local copies, waits for them, and re-layouts: 33.4 us -> none  [the longest x4 16.8 us: visit_tile(): value_tiles = jnp.take(value_blocks, picked, axis=0)]
  transfers between devices with their start and end apart: 6 -> 5, of which waited for: 6 -> 3; matrix products, arithmetic and copies ran while one was open for 1% -> 12% of each run, Pallas kernels for 0% -> 24%
where the time goes in v1:
time: 256 us; the launch traced here: 255 us
  waiting for transfers between devices  116 us (45%)
  Pallas kernels  62.4 us (24%)
  matrix products  33.7 us (13%)
  between operations  13.9 us (5%)
  blocking collectives  12.4 us (5%)
  other arithmetic  7.95 us (3%)
  starting transfers between devices  4.48 us (2%)
  local copies, waits for them, and re-layouts  4.18 us (2%)
    all_gather x1, waiting for transfers between devices, local(): down_all = lax.all_gather(w_down, 'qrow', axis=0)  56.2 us
    pallas_call x1, Pallas kernels, edge_stage(): pl.pallas_call(edge_kernel, grid_spec=grid_spec, out_shape=[jax.ShapeDtyp...  32.9 us
    all_gather x1, waiting for transfers between devices, local(): column_nodes = lax.all_gather(normed, 'qrow', axis=0)  31.8 us
    pallas_call x1, Pallas kernels, attend_stage(): pl.pallas_call(attend_kernel, grid_spec=grid_spec, out_shape=[jax.ShapeDt...  29.5 us
    all_to_all x1, waiting for transfers between devices, local(): partial = lax.all_to_all(partial, 'kcol', 0, 0, tiled=True)  26.3 us
    all_to_all x1, blocking collectives, local(): stats = lax.all_to_all(stats, 'kcol', 0, 0, tiled=True)  12.4 us
    dot_general x1, matrix products, local(): jnp.einsum('snf,sfd->nd', hidden, down_all, preferred_element_type=jnp.fl...  11.4 us
    dot_general x1, matrix products, local(): jnp.einsum('kd,gnk->gdn', w_value, column_nodes, preferred_element_type=j...  7.9 us
  transfers between devices with their start and end apart: 5, of which 3 were waited for; matrix products, arithmetic and copies ran while one was open for 12% of the time, Pallas kernels for 24%

profile of v1, /device:TPU:1, one launch (start us, length us, event | category | flops | bytes accessed | tf_op | source)
XLA Modules:
  0.0 255.2 jit_solution(17997417238595273876)
XLA Ops:
  6.6 1.8 fusion.105
  8.7 0.9 multiply_convert_fusion.1
  9.6 0.7 all-gather.9.cloned.1.call-update
  10.4 0.7 all-gather.13.cloned.1.call-update
  12.4 0.7 convert_reduce_fusion
  13.2 1.0 mul.113.mix_ref
  14.3 0.8 convert_reduce_fusion.2
  15.8 0.8 select_reduce_fusion
  16.6 1.2 fusion.74.live_of
  17.9 1.2 fusion.72.last_of
  19.0 1.1 fusion.73.first_of
  20.8 0.7 broadcast_in_dim.105.shift_ref
  21.5 32.9 %edge_terms.1 = (f32[32,16,128,128]{3,2,1,0:T(8,128)}, bf16[32,16,128,128]{3,2,1,0:T(8,128)(2,1)}) custom-call(s32[32]{0:T(128)} %get-tuple-element.13.tile_of, s32[32]{0:T(128)} %copy-done.4, s32[32]{0:T(128)} %fusion.74.live_of, f32[16]{0:T(128)} %slopes.1, f32[32]{0:T(128)} %get-tuple-element.19.offsets, bf16[32,128,128]{2,1,0:T(8,128)(2,1)} %bitcast.131, ...), custom_call_target="tpu_custom_call" | custom-call | flops 17179869184 | bytes 50331648 | tf_op jit(solution)/shard_map/edge_terms/pallas_call | solution.py:95
  54.4 6.0 %multiply_bitcast_fusion.query_ref = bf16[8,1024,128]{2,1,0:T(8,128)(2,1)} fusion(bf16[8,128,1024]{2,1,0:T(8,128)(2,1)} %bitcast.130, bf16[1024,1024]{1,0:T(8,128)(2,1)} %param.19), kind=kOutput, calls=%fused_computation.30 | convolution fusion | flops 2149580800 | bytes 6291456 | tf_op jit(solution)/shard_map/kd,gnk->gdn/dot_general | solution.py:321
  60.4 31.8 %all-gather.9.cloned.1.call-done = bf16[2048,1024]{1,0:T(8,128)(2,1)} async-done(((bf16[128,1024]{1,0:T(8,128)(2,1)}), bf16[2048,1024]{1,0:T(8,128)(2,1)}) %all-gather.9.cloned.1.call-update) | async-done | bytes 4194320 | tf_op jit(solution)/shard_map/all_gather | solution.py:300
  92.2 7.9 %convert_bitcast_fusion.value_ref = bf16[16,1024,128]{2,1,0:T(8,128)(2,1)} fusion(bf16[16,128,1024]{2,1,0:T(8,128)(2,1)} %bitcast.128, bf16[1024,1024]{1,0:T(8,128)(2,1)S(1)} %copy-done), kind=kOutput, calls=%fused_computation.2 | convolution fusion | flops 4297064448 | bytes 10485760 | tf_op jit(solution)/shard_map/kd,gnk->gdn/dot_general | solution.py:329
  100.1 6.0 %convolution_convert_fusion.key_ref = bf16[16,128,1024]{2,1,0:T(8,128)(2,1)} fusion(bf16[16,128,1024]{2,1,0:T(8,128)(2,1)S(1)} %bitcast.129, bf16[1024,1024]{1,0:T(8,128)(2,1)S(1)} %copy-done.8), kind=kOutput, calls=%fused_computation.4 | convolution fusion | flops 4297064448 | bytes 10485760 | tf_op jit(solution)/shard_map/gnk,kd->gnd/dot_general | solution.py:326
  106.1 29.5 %attend.1 = (bf16[8,1024,128]{2,1,0:T(8,128)(2,1)}, f32[8,32,128]{2,1,0:T(8,128)}) custom-call(s32[32]{0:T(128)} %copy-done.4, s32[32]{0:T(128)} %get-tuple-element.18.block_of, s32[32]{0:T(128)} %get-tuple-element.17.key_of, s32[32]{0:T(128)} %fusion.74.live_of, s32[32]{0:T(128)} %fusion.73.first_of, s32[32]{0:T(128)} %fusion.72.last_of, ...), custom_call_target="tpu_custom_call" | custom-call | flops 2147483648 | bytes 50331648 | tf_op jit(solution)/shard_map/attend/pallas_call | solution.py:215
  135.6 12.4 %all_to_all.10 = f32[8,32,128]{2,1,0:T(8,128)S(1)} all-to-all(f32[8,32,128]{2,1,0:T(8,128)} %get-tuple-element.12), channel_id=1, replica_groups=mesh['qrow'=16,'kcol'=8] {'kcol'}, dimensions={0} | all-to-all | bytes 262144 | tf_op jit(solution)/shard_map/all_to_all | solution.py:336
  148.0 4.3 %all-to-all-start = ((bf16[8,1024,128]{2,1,0:T(8,128)(2,1)}), bf16[8,1024,128]{2,1,0:T(8,128)(2,1)S(1)}, u32[]{:S(2)}, u32[]{:S(2)}) async-start(bf16[8,1024,128]{2,1,0:T(8,128)(2,1)} %get-tuple-element.11), calls=%async_computation | async-start | bytes 4194304 | tf_op jit(solution)/shard_map/all_to_all | solution.py:335
  152.4 26.3 %all-to-all-done = bf16[8,1024,128]{2,1,0:T(8,128)(2,1)S(1)} async-done(((bf16[8,1024,128]{2,1,0:T(8,128)(2,1)}), bf16[8,1024,128]{2,1,0:T(8,128)(2,1)S(1)}, u32[]{:S(2)}, u32[]{:S(2)}) %all-to-all-start) | async-done | bytes 2097184 | tf_op jit(solution)/shard_map/all_to_all | solution.py:335
  179.1 1.2 copy-done.2
  181.1 56.2 %all-gather.15.cloned.1.call-done = bf16[4096,1024]{1,0:T(8,128)(2,1)} async-done(((bf16[256,1024]{1,0:T(8,128)(2,1)}), bf16[4096,1024]{1,0:T(8,128)(2,1)}) %all-gather.15.cloned.1.call-update) | async-done | bytes 8388624 | tf_op jit(solution)/shard_map/all_gather | solution.py:302
  237.3 11.4 %fusion.26 = bf16[128,1024]{1,0:T(8,128)(2,1)} fusion(f32[128,1024]{1,0:T(8,128)S(1)} %get-tuple-element.26, bf16[16,256,1024]{2,1,0:T(8,128)(2,1)} %bitcast.127, bf16[16,1024,256]{2,1,0:T(8,128)(2,1)} %bitcast.126, f32[128]{0:T(128)S(1)} %add_rsqrt_fusion, f32[128]{0:T(128)S(1)} %broadcast_multiply_fusion.1), kind=kOutput, calls=%fused_computation.37 | convolution fusion | flops 2182217728 | bytes 17564672 | tf_op jit(solution)/shard_map/snf,sfd->nd/dot_general | solution.py:351
  (61 shorter events, 3.8 us)
Async XLA Ops:
  6.5 85.7 %copy-start = (bf16[1024,1024]{1,0:T(8,128)(2,1)S(1)}, bf16[1024,1024]{1,0:T(8,128)(2,1)}, u32[]{:S(2)}) copy-start(bf16[1024,1024]{1,0:T(8,128)(2,1)} %param.21) | copy-start | bytes 6291460
  6.5 5.1 %copy-start.6 = (s32[8,1]{0,1:T(1,128)S(1)}, s32[8,1]{0,1:T(1,128)}, u32[]{:S(2)}) copy-start(s32[8,1]{0,1:T(1,128)} %param.29) | copy-start | bytes 100
  6.5 5.5 %copy-start.5 = (s32[8,1,4]{0,2,1:T(4,128)S(1)}, s32[8,1,4]{0,2,1:T(4,128)}, u32[]{:S(2)}) copy-start(s32[8,1,4]{0,2,1:T(4,128)} %param.28) | copy-start | bytes 388
  6.5 5.9 %copy-start.3 = (bf16[64,32]{0,1:T(8,128)(2,1)S(1)}, bf16[64,32]{0,1:T(8,128)(2,1)}, u32[]{:S(2)}) copy-start(bf16[64,32]{0,1:T(8,128)(2,1)} %param.26) | copy-start | bytes 12292
  6.5 47.9 %all-gather.11.cloned.1.call-start = ((), (), s32[]{:S(2)}) async-start(), calls=%async_computation.3 | async-start | bytes 2359296 | tf_op jit(solution)/shard_map/all_gather | solution.py:299
  8.4 9.4 %copy-start.9 = (f32[64]{0:T(128)S(1)}, f32[64]{0:T(128)}, u32[]{:S(2)}) copy-start(f32[64]{0:T(128)} %param.24) | copy-start | bytes 772
  8.4 9.4 %copy-start.10 = (f32[64]{0:T(128)S(1)}, f32[64]{0:T(128)}, u32[]{:S(2)}) copy-start(f32[64]{0:T(128)} %param.25) | copy-start | bytes 772
  9.6 82.6 %all-gather.9.cloned.1.call-start = ((), (), s32[]{:S(2)}) async-start(), calls=%async_computation.2 | async-start | bytes 4456448 | tf_op jit(solution)/shard_map/all_gather | solution.py:300
  10.3 170.8 %all-gather.13.cloned.1.call-start = ((), (), s32[]{:S(2)}) async-start(), calls=%async_computation.4 | async-start | bytes 8912896 | tf_op jit(solution)/shard_map/all_gather | solution.py:301
  11.0 226.2 %all-gather.15.cloned.1.call-start = ((), (), s32[]{:S(2)}) async-start(), calls=%async_computation.5 | async-start | bytes 8912896 | tf_op jit(solution)/shard_map/all_gather | solution.py:302
  15.7 5.8 %copy-start.4 = (s32[32]{0:T(128)}, s32[32]{0:T(128)S(1)}, u32[]{:S(2)}) copy-start(s32[32]{0:T(128)S(1)} %iota_minimum_fusion.slot_of) | copy-start | bytes 388
  92.2 7.9 %copy-start.7 = (bf16[2048,1024]{1,0:T(8,128)(2,1)S(1)}, bf16[2048,1024]{1,0:T(8,128)(2,1)}, u32[]{:S(2)}) copy-start(bf16[2048,1024]{1,0:T(8,128)(2,1)} %all-gather.9.cloned.1.call-done) | copy-start | bytes 12582916
  92.2 7.9 %copy-start.8 = (bf16[1024,1024]{1,0:T(8,128)(2,1)S(1)}, bf16[1024,1024]{1,0:T(8,128)(2,1)}, u32[]{:S(2)}) copy-start(bf16[1024,1024]{1,0:T(8,128)(2,1)} %param.20) | copy-start | bytes 6291460
  148.0 30.7 %all-to-all-start = ((bf16[8,1024,128]{2,1,0:T(8,128)(2,1)}), bf16[8,1024,128]{2,1,0:T(8,128)(2,1)S(1)}, u32[]{:S(2)}, u32[]{:S(2)}) async-start(bf16[8,1024,128]{2,1,0:T(8,128)(2,1)} %get-tuple-element.11), calls=%async_computation | async-start | bytes 4194304 | tf_op jit(solution)/shard_map/all_to_all | solution.py:335
  178.7 1.6 copy-start.2
  237.3 11.4 %copy-start.1 = (bf16[1024,1024]{1,0:T(8,128)(2,1)S(1)}, bf16[1024,1024]{1,0:T(8,128)(2,1)}, u32[]{:S(2)}) copy-start(bf16[1024,1024]{1,0:T(8,128)(2,1)} %param.21) | copy-start | bytes 6291460
Sparse Core Ops, SparseCore 0:
  9.7 28.7 all-gather.10
  40.6 51.5 all-gather.8
  94.3 70.4 all-gather.12
  166.8 70.4 all-gather.14

commit v2 on v1

v2 whole, which is shorter than its diff:
```python
import functools

import jax
import jax.numpy as jnp
from jax import lax
from jax.experimental import pallas as pl
from jax.experimental.pallas import tpu as pltpu
from jax.sharding import PartitionSpec as P

NEG_FILL = -1e30
CUTS = (6, 11, 22)
EDGE_VMEM = 56 * 1024 * 1024
ATTEND_VMEM = 56 * 1024 * 1024
TAIL_VMEM = 24 * 1024 * 1024


def layer_norm(values):
    average = jnp.mean(values, axis=-1, keepdims=True)
    centered = values - average
    spread = jnp.mean(centered * centered, axis=-1, keepdims=True)
    return centered * lax.rsqrt(spread + 1e-05)


def list_kernel(counts_ref, index_ref, place_ref, lists_ref):
    block_total, slot_count = index_ref.shape
    total = block_total * slot_count
    row_hi, row_lo, col_hi, col_lo = place_ref[0], place_ref[1], place_ref[2], place_ref[3]

    def relative(theirs, ours):
        gap = (theirs - ours + 4) & 3
        return jnp.where(gap == 0, 0, jnp.where(gap == 3, 1, gap + 1))

    filled = jnp.int32(0)
    for block in range(block_total):
        count = counts_ref[block, 0]
        other = jnp.where(col_lo == block % 2, 0, 4)
        partner = other + relative(jnp.int32(block // 2), col_hi)
        visits = jnp.maximum(count, 1)
        for slot in range(slot_count):

            @pl.when(slot < visits)
            def _(at=filled, block=block, slot=slot, partner=partner, count=count, visits=visits):
                key_block = index_ref[block, slot]
                lists_ref[0, at] = jnp.int32(block * slot_count + slot)
                lists_ref[1, at] = at
                lists_ref[2, at] = partner
                lists_ref[3, at] = 4 * relative(key_block >> 2, row_hi) + relative(
                    key_block & 3, row_lo
                )
                lists_ref[4, at] = (slot < count).astype(jnp.int32)
                lists_ref[5, at] = jnp.int32(slot == 0)
                lists_ref[6, at] = (visits == slot + 1).astype(jnp.int32)

            filled = filled + (slot < visits).astype(jnp.int32)

    @pl.loop(0, total)
    def _(step):
        @pl.when(step >= filled)
        def _():
            for row in range(4):
                lists_ref[row, step] = lists_ref[row, filled - 1]
            for row in range(4, 7):
                lists_ref[row, step] = jnp.int32(0)


def list_stage(counts, index, place):
    scalars = pl.BlockSpec(memory_space=pltpu.SMEM)
    return pl.pallas_call(
        list_kernel,
        in_specs=[scalars] * 3,
        out_specs=scalars,
        out_shape=jax.ShapeDtypeStruct((8, index.shape[0] * index.shape[1]), jnp.int32),
        name="lists",
    )(counts, index, place)


def edge_kernel(start, lists, offsets, edge_ref, mix_ref, scale_ref, shift_ref, *rest):
    bias_ref, gate_ref, edge_t, chans = rest[-4:]
    step = pl.program_id(0) + start
    heads = bias_ref.shape[1]
    rows, lanes = edge_t.shape
    channel_count = scale_ref.shape[0]

    @pl.when(lists[4, step] > 0)
    def _():
        edge_t[...] = edge_ref[0].astype(jnp.float32).T
        scale = scale_ref[...]
        shift = shift_ref[...]
        for part in range(rows // 16):
            slot = part % 2
            for half in range(2):
                for within in range(8):
                    row = part * 16 + half * 8 + within
                    line = jnp.broadcast_to(edge_t[row : row + 1, :], scale.shape)
                    pre = (line * scale + shift).astype(jnp.bfloat16)
                    chans[
                        slot,
                        within * channel_count : (within + 1) * channel_count,
                        half * lanes : (half + 1) * lanes,
                    ] = jnp.tanh(pre)
            terms = jnp.dot(mix_ref[...], chans[slot], preferred_element_type=jnp.float32)
            span = slice(part * 16, part * 16 + 16)
            for head in range(heads):
                block = terms[head * 8 : head * 8 + 8]
                both = jnp.concatenate([block[:, :lanes], block[:, lanes:]], axis=0)
                bias_ref[0, head, span, :] = both.astype(jnp.bfloat16)
                block = terms[(heads + head) * 8 : (heads + head) * 8 + 8]
                both = jnp.concatenate([block[:, :lanes], block[:, lanes:]], axis=0)
                gate_ref[0, head, span, :] = (
                    0.5 + 0.5 * jnp.tanh(both + offsets[heads + head])
                ).astype(jnp.bfloat16)


def edge_stage(start, stop, lists, offsets, edges, mix, scale, shift, heads, held):
    tiles, rows, lanes = edges.shape
    out = pl.BlockSpec((1, heads, rows, lanes), lambda s, lists, *_: (jnp.maximum(lists[1, s + start], start), 0, 0, 0))
    grid_spec = pltpu.PrefetchScalarGridSpec(
        num_scalar_prefetch=2,
        grid=(stop - start,),
        in_specs=[
            pl.BlockSpec((1, rows, lanes), lambda s, lists, *_: (lists[0, s + start], 0, 0)),
            pl.BlockSpec(mix.shape, lambda s, *_: (0, 0)),
            pl.BlockSpec(scale.shape, lambda s, *_: (0, 0)),
            pl.BlockSpec(shift.shape, lambda s, *_: (0, 0)),
        ]
        + [pl.BlockSpec(memory_space=pl.ANY)] * len(held),
        out_specs=[out, out],
        scratch_shapes=[
            pltpu.VMEM((rows, lanes), jnp.float32),
            pltpu.VMEM((2, mix.shape[1], 2 * lanes), jnp.bfloat16),
        ],
    )
    count = stop - start
    return pl.pallas_call(
        functools.partial(edge_kernel, start),
        grid_spec=grid_spec,
        out_shape=[jax.ShapeDtypeStruct((tiles, heads, rows, lanes), jnp.bfloat16)] * 2,
        input_output_aliases={6: 0, 7: 1} if held else {},
        compiler_params=pltpu.CompilerParams(vmem_limit_bytes=EDGE_VMEM),
        cost_estimate=pl.CostEstimate(
            flops=count * 2 * rows * lanes * 64 * 256 * 2,
            bytes_accessed=count * rows * lanes * heads * 4,
            transcendentals=count * rows * lanes * 80,
        ),
        name="edge_terms",
    )(lists, offsets, edges, mix, scale, shift, *held)


def attend_kernel(
    lists,
    slopes,
    offsets,
    edge_ref,
    bias_ref,
    gate_ref,
    key_ref,
    value_ref,
    query_ref,
    num_ref,
    stat_ref,
    query_pairs,
    acc,
    tops,
    totals,
):
    step = pl.program_id(0)
    heads, rows, lanes = bias_ref.shape[1:]
    head_dim = acc.shape[0] // heads

    @pl.when(lists[5, step] > 0)
    def _():
        block = lists[2, step]
        acc[...] = jnp.zeros_like(acc)
        tops[...] = jnp.full_like(tops, NEG_FILL)
        totals[...] = jnp.zeros_like(totals)
        blank = jnp.zeros((head_dim, lanes), jnp.bfloat16)
        for pair in range(heads // 2):
            upper = query_ref[block, pair * 2 * head_dim : (pair * 2 + 1) * head_dim, :]
            lower = query_ref[block, (pair * 2 + 1) * head_dim : (pair * 2 + 2) * head_dim, :]
            query_pairs[pair, :head_dim, :lanes] = upper
            query_pairs[pair, :head_dim, lanes:] = blank
            query_pairs[pair, head_dim:, :lanes] = blank
            query_pairs[pair, head_dim:, lanes:] = lower

    @pl.when(lists[4, step] > 0)
    def _():
        key_block = lists[3, step]
        edge_t = edge_ref[0].astype(jnp.float32).T
        for pair in range(heads // 2):
            width = 2 * head_dim
            keys = key_ref[key_block, :, pair * width : (pair + 1) * width]
            both = jnp.dot(keys, query_pairs[pair], preferred_element_type=jnp.float32)
            for side in range(2):
                head = pair * 2 + side
                span = slice(head * head_dim, (head + 1) * head_dim)
                scores = both[:, side * lanes : (side + 1) * lanes] + (
                    bias_ref[0, head].astype(jnp.float32) + (edge_t * slopes[head] + offsets[head])
                )
                old_top = tops[head : head + 1, :]
                new_top = jnp.maximum(old_top, jnp.max(scores, axis=0, keepdims=True))
                factor = jnp.exp(old_top - new_top)
                weights = jnp.exp(scores - new_top)
                totals[head : head + 1, :] = totals[head : head + 1, :] * factor + jnp.sum(
                    weights, axis=0, keepdims=True
                )
                tops[head : head + 1, :] = new_top
                gated = (weights * gate_ref[0, head].astype(jnp.float32)).astype(jnp.bfloat16)
                part = jnp.dot(
                    value_ref[key_block, span, :], gated, preferred_element_type=jnp.float32
                )
                acc[span, :] = acc[span, :] * factor + part

    @pl.when(lists[6, step] > 0)
    def _():
        for head in range(heads):
            span = slice(head * head_dim, (head + 1) * head_dim)
            total = totals[head : head + 1, :]
            inverse = jnp.where(total > 0.0, 1.0 / jnp.where(total > 0.0, total, 1.0), 0.0)
            num_ref[0, span, :] = (acc[span, :] * inverse).astype(num_ref.dtype)
        stat_ref[0, :heads, :] = tops[...]
        stat_ref[0, heads:, :] = totals[...]


def attend_stage(lists, slopes, offsets, edges, bias, gate, keys, values, queries):
    block_total, width, lanes = queries.shape
    tiles, heads, rows, _ = bias.shape
    whole = lambda array: pl.BlockSpec(
        array.shape, lambda s, *_: (0,) * array.ndim, pipeline_mode=pl.Buffered(1)
    )
    edge_block = pl.BlockSpec((1, heads, rows, lanes), lambda s, lists, *_: (lists[1, s], 0, 0, 0))
    grid_spec = pltpu.PrefetchScalarGridSpec(
        num_scalar_prefetch=3,
        grid=(tiles,),
        in_specs=[
            pl.BlockSpec((1, rows, lanes), lambda s, lists, *_: (lists[0, s], 0, 0)),
            edge_block,
            edge_block,
            whole(keys),
            whole(values),
            whole(queries),
        ],
        out_specs=[
            pl.BlockSpec((1, width, lanes), lambda s, lists, *_: (lists[2, s], 0, 0)),
            pl.BlockSpec((1, 2 * heads, lanes), lambda s, lists, *_: (lists[2, s], 0, 0)),
        ],
        scratch_shapes=[
            pltpu.VMEM((heads // 2, 2 * width // heads, 2 * lanes), jnp.bfloat16),
            pltpu.VMEM((width, lanes), jnp.float32),
            pltpu.VMEM((heads, lanes), jnp.float32),
            pltpu.VMEM((heads, lanes), jnp.float32),
        ],
    )
    return pl.pallas_call(
        attend_kernel,
        grid_spec=grid_spec,
        out_shape=[
            jax.ShapeDtypeStruct((block_total, width, lanes), jnp.bfloat16),
            jax.ShapeDtypeStruct((block_total, 2 * heads, lanes), jnp.float32),
        ],
        compiler_params=pltpu.CompilerParams(vmem_limit_bytes=ATTEND_VMEM),
        cost_estimate=pl.CostEstimate(
            flops=tiles * 16 * rows * lanes * width,
            bytes_accessed=tiles * rows * lanes * heads * 4,
            transcendentals=tiles * rows * lanes * heads,
        ),
        name="attend",
    )(lists, slopes, offsets, edges, bias, gate, keys, values, queries)


def merge_parts(parts, stats, heads):
    top = stats[0][:heads]
    for stat in stats[1:]:
        top = jnp.maximum(top, stat[:heads])
    shares = [stat[heads:] * jnp.exp(stat[:heads] - top) for stat in stats]
    total = sum(shares[1:], shares[0])
    live = total > 0.0
    inverse = jnp.where(live, 1.0 / jnp.where(live, total, 1.0), 0.0)
    return top, total, [share * inverse for share in shares]


def merge_kernel(own_ref, other_ref, own_stat, other_stat, num_ref, stat_ref):
    heads = own_stat.shape[1] // 2
    head_dim = own_ref.shape[1] // heads
    top, total, shares = merge_parts(None, [own_stat[0], other_stat[0]], heads)
    for head in range(heads):
        span = slice(head * head_dim, (head + 1) * head_dim)
        num_ref[0, span, :] = (
            own_ref[0, span, :].astype(jnp.float32) * shares[0][head : head + 1]
            + other_ref[0, span, :].astype(jnp.float32) * shares[1][head : head + 1]
        ).astype(num_ref.dtype)
    stat_ref[0, :heads, :] = top
    stat_ref[0, heads:, :] = total


def merge_stage(own, other, own_stat, other_stat):
    count, width, lanes = other.shape
    stat_rows = other_stat.shape[1]
    block = pl.BlockSpec((1, width, lanes), lambda s: (s, 0, 0))
    stat = pl.BlockSpec((1, stat_rows, lanes), lambda s: (s, 0, 0))
    return pl.pallas_call(
        merge_kernel,
        grid=(count,),
        in_specs=[block, block, stat, stat],
        out_specs=[block, stat],
        out_shape=[
            jax.ShapeDtypeStruct((count, width, lanes), jnp.bfloat16),
            jax.ShapeDtypeStruct((count, stat_rows, lanes), jnp.float32),
        ],
        name="merge",
    )(own, other, own_stat, other_stat)


def tail_kernel(
    core,
    part_0,
    part_1,
    part_2,
    part_3,
    stat_0,
    stat_1,
    stat_2,
    stat_3,
    embedded_ref,
    out_ref,
    own_ref,
    other_ref,
    final_ref,
    attended,
    residual,
    normed,
    acc,
):
    step = pl.program_id(0)

    @pl.when(step == 0)
    def _():
        heads = stat_0.shape[1] // 2
        head_dim = attended.shape[0] // heads
        parts = [part_0, part_1, part_2, part_3]
        stats = [stat[0] for stat in (stat_0, stat_1, stat_2, stat_3)]
        _, _, shares = merge_parts(None, stats, heads)
        for head in range(heads):
            span = slice(head * head_dim, (head + 1) * head_dim)
            merged = parts[0][0, span, :].astype(jnp.float32) * shares[0][head : head + 1]
            for part, share in zip(parts[1:], shares[1:]):
                merged = merged + part[0, span, :].astype(jnp.float32) * share[head : head + 1]
            attended[span, :] = merged
        rows = attended[...].T.astype(jnp.bfloat16)
        values = embedded_ref[...] + jnp.dot(
            rows, out_ref[...], preferred_element_type=jnp.float32
        )
        residual[...] = values
        normed[...] = layer_norm(values).astype(jnp.bfloat16)
        acc[...] = jnp.zeros_like(acc)

    def feed(up_ref, down_ref):
        pre = jnp.dot(normed[...], up_ref[0], preferred_element_type=jnp.float32)
        hidden = (0.5 * pre * (1.0 + lax.erf(pre * (0.5**0.5)))).astype(jnp.bfloat16)
        span = hidden.shape[1]
        for piece in range(acc.shape[1] // span):
            cut = slice(piece * span, (piece + 1) * span)
            acc[:, cut] += jnp.dot(hidden, down_ref[0, cut, :], preferred_element_type=jnp.float32)

    @pl.when(core[0] == 0)
    def _():
        feed(own_ref, other_ref)

    @pl.when(core[0] != 0)
    def _():
        feed(other_ref, own_ref)

    @pl.when(step == pl.num_programs(0) - 1)
    def _():
        final_ref[...] = (residual[...] + acc[...]).astype(final_ref.dtype)


def tail_stage(core, parts, stats, embedded, w_out, own, other):
    shards, width, span = own.shape
    rows = embedded.shape[0]
    lanes = parts[0].shape[2]
    part = pl.BlockSpec((1, width, lanes), lambda s, *_: (0, 0, 0))
    stat = pl.BlockSpec((1, stats[0].shape[1], lanes), lambda s, *_: (0, 0, 0))
    weight = pl.BlockSpec((1, width, span), lambda s, *_: (s, 0, 0))
    flat = lambda array: pl.BlockSpec(array.shape, lambda s, *_: (0, 0))
    grid_spec = pltpu.PrefetchScalarGridSpec(
        num_scalar_prefetch=1,
        grid=(shards,),
        in_specs=[part] * 4 + [stat] * 4 + [flat(embedded), flat(w_out), weight, weight],
        out_specs=pl.BlockSpec((rows, width), lambda s, *_: (0, 0)),
        scratch_shapes=[
            pltpu.VMEM((width, lanes), jnp.float32),
            pltpu.VMEM((rows, width), jnp.float32),
            pltpu.VMEM((rows, width), jnp.bfloat16),
            pltpu.VMEM((rows, width), jnp.float32),
        ],
    )
    return pl.pallas_call(
        tail_kernel,
        grid_spec=grid_spec,
        out_shape=jax.ShapeDtypeStruct((rows, width), jnp.bfloat16),
        compiler_params=pltpu.CompilerParams(vmem_limit_bytes=TAIL_VMEM),
        cost_estimate=pl.CostEstimate(
            flops=4 * rows * width * span * shards,
            bytes_accessed=2 * shards * width * span * 2,
            transcendentals=rows * span * shards,
        ),
        name="tail",
    )(core, *parts, *stats, embedded, w_out, own, other)


def mix_matrix(edge_proj, heads):
    channel_count, outs = edge_proj.shape
    factors = jnp.where(jnp.arange(outs) < heads, 0.5, 0.25).astype(jnp.bfloat16)
    scaled = (edge_proj * factors[None, :]).T
    eye = jnp.eye(8, dtype=jnp.bfloat16)
    mixed = scaled[:, None, None, :] * eye[None, :, :, None]
    offsets = jnp.sum(scaled.astype(jnp.float32), axis=1)
    return mixed.reshape(outs * 8, 8 * channel_count), offsets


def shift_low(value, by):
    return lax.ppermute(value, "qrow", [(i, (i & 12) | ((i + by) & 3)) for i in range(16)])


def shift_high(value, by):
    return lax.ppermute(value, "qrow", [(i, (i + 4 * by) & 15) for i in range(16)])


def shift_chip(value, by):
    return lax.ppermute(value, "kcol", [(i, (i + 2 * by) & 7) for i in range(8)])


def after(value, others):
    return lax.optimization_barrier((value, others))[0]


def swap_core(value):
    return lax.ppermute(value, "kcol", [(i, i ^ 1) for i in range(8)])


def local(
    features,
    node_ids,
    token_embed,
    w_query,
    w_key,
    w_value,
    w_out,
    slopes,
    chan_scale,
    chan_shift,
    edge_proj,
    edge_value,
    key_index,
    counts,
    w_up,
    w_down,
):
    node_dev, width = features.shape
    vocab_size = token_embed.shape[0]
    heads = slopes.shape[0]
    head_dim = width // heads
    rows = edge_value.shape[-1]
    row_at = lax.axis_index("qrow")
    col_at = lax.axis_index("kcol")
    core = col_at & 1

    span = w_up.shape[1]
    down_stack = jnp.concatenate(
        [w_down[:, cut : cut + span] for cut in range(0, width, span)], axis=0
    )
    own_weights = lax.all_gather(jnp.where(core == 0, w_up, down_stack), "qrow", axis=0)

    one_hot = (
        node_ids[:, None] == lax.broadcasted_iota(jnp.int32, (node_dev, vocab_size), 1)
    ).astype(jnp.bfloat16)
    embedded = features.astype(jnp.float32) + jnp.dot(
        one_hot, token_embed, preferred_element_type=jnp.float32
    )
    normed = layer_norm(embedded).astype(jnp.bfloat16)

    half = node_dev // 2
    first = [normed[:half], normed[half:]]
    axes = [(shift_low, shift_high), (shift_high, shift_low)]
    near = [[move[0](part, 1), move[0](part, -1)] for part, move in zip(first, axes)]
    row_near = [shift_chip(normed, 1)]

    lists = list_stage(
        counts, key_index[:, 0], jnp.stack([row_at >> 2, row_at & 3, col_at >> 1, core])
    )
    mix, offsets = mix_matrix(edge_proj, heads)
    spread = lambda vector: jnp.broadcast_to((0.5 * vector)[:, None], (vector.shape[0], rows))
    edges = edge_value.reshape(-1, rows, rows)
    scale, shift = spread(chan_scale), spread(chan_shift)

    def edge_part(start, stop, held, others):
        pinned = after(lists, others)
        return edge_stage(start, stop, pinned, offsets, edges, mix, scale, shift, heads, held)

    held = edge_part(0, CUTS[0], (), normed)
    far = [
        [move[0](pair[0][: half // 2], 1), move[0](pair[1][half // 2 :], -1)]
        for pair, move in zip(near, axes)
    ]
    held = edge_part(CUTS[0], CUTS[1], held, (near, row_near))
    row_near.append(shift_chip(after(normed, near), -1))
    lines = [
        jnp.concatenate([part, *pair, *ends], axis=0) for part, pair, ends in zip(first, near, far)
    ]
    near = [[move[1](line, 1), move[1](line, -1)] for line, move in zip(lines, axes)]
    held = edge_part(CUTS[1], CUTS[2], held, (far, row_near))
    row_near.append(shift_chip(after(normed, far), 2))
    cut = 2 * half
    far = [
        [move[1](pair[0][:cut], 1), move[1](pair[1][cut:], -1)] for pair, move in zip(near, axes)
    ]
    bias, gate = edge_part(CUTS[2], edges.shape[0], held, (near, row_near))
    row_own = jnp.concatenate([normed, *row_near], axis=0)
    row_other = swap_core(row_own)
    planes = [
        jnp.concatenate([line, *pair, *ends], axis=0).reshape(4, 4, half, width)
        for line, pair, ends in zip(lines, near, far)
    ]
    column_nodes = jnp.concatenate([planes[0], jnp.swapaxes(planes[1], 0, 1)], axis=2).reshape(
        16, node_dev, width
    )
    row_nodes = jnp.concatenate([row_own, row_other], axis=0).reshape(
        8, node_dev, width
    )
    queries = (
        jnp.einsum("kd,gnk->gdn", w_query, row_nodes, preferred_element_type=jnp.float32).astype(
            jnp.bfloat16
        )
        * jnp.bfloat16(head_dim ** (-0.5))
    )
    keys = jnp.einsum(
        "gnk,kd->gnd", column_nodes, w_key, preferred_element_type=jnp.float32
    ).astype(jnp.bfloat16)
    values = jnp.einsum(
        "kd,gnk->gdn", w_value, column_nodes, preferred_element_type=jnp.float32
    ).astype(jnp.bfloat16)
    part, stat = attend_stage(lists, slopes, offsets, edges, bias, gate, keys, values, queries)
    own_weights, part = lax.optimization_barrier((own_weights, part))
    other_weights = swap_core(own_weights)
    part, stat = merge_stage(part, swap_core(part[4:]), stat, swap_core(stat[4:]))
    parts, stats = [part], [stat]
    for at, step in ((1, -1), (2, 1), (3, 2)):
        parts.append(shift_chip(part[at : at + 1], step))
        stats.append(shift_chip(stat[at : at + 1], step))
    return tail_stage(
        core.reshape(1), parts, stats, embedded, w_out, own_weights, other_weights
    )


def solution(mesh):
    placed = (
        P(("qrow", "kcol"), None),
        P(("qrow", "kcol")),
        P(),
        P(),
        P(),
        P(),
        P(),
        P(),
        P(),
        P(),
        P(),
        P("qrow", "kcol", None, None, None),
        P("qrow", "kcol", None),
        P("qrow", "kcol"),
        P(None, "qrow"),
        P("qrow", None),
    )
    return jax.shard_map(
        local, mesh=mesh, in_specs=placed, out_specs=P(("qrow", "kcol"), None), check_vma=False
    )
```

time: 256 us -> 250 us (0.977); the launches traced: 255 us -> 245 us
  waiting for transfers between devices: 116 us -> 29.3 us
  starting transfers between devices: 4.48 us -> 61 us
  local copies, waits for them, and re-layouts: 4.18 us -> 41.4 us
  matrix products: 33.7 us -> 20.7 us
  blocking collectives: 12.4 us -> 0 us
  Pallas kernels: 62.4 us -> 73.7 us
    all_gather x4 -> x1, waiting for transfers between devices: 88 us -> 0.02 us  [local(): lax.all_gather(jnp.where(core == 0, w_up, down_stack), 'qrow', axis=0)]
    ppermute x0 -> x29, starting transfers between devices: none -> 61 us  [the longest x4 28 us: swap_core(): return lax.ppermute(value, 'kcol', [(i, i ^ 1) for i in range(8)])]
    ppermute x0 -> x29, waiting for transfers between devices: none -> 29.2 us  [the longest x9 16.8 us: shift_chip(): return lax.ppermute(value, 'kcol', [(i, i + 2 * by & 7) for i in range(8)])]
    all_to_all x1 -> x0, waiting for transfers between devices: 26.3 us -> none  [local(): partial = lax.all_to_all(partial, 'kcol', 0, 0, tiled=True)]
    unnamed x23 -> x59, local copies, waits for them, and re-layouts: 1.3 us -> 25.3 us
    pallas_call x1 -> x7, Pallas kernels: 32.9 us -> 51.2 us  [the longest x4 29.9 us: edge_stage(): pl.pallas_call(functools.partial(edge_kernel, start), grid_spec=grid_spec...]
    all_to_all x1 -> x0, blocking collectives: 12.4 us -> none  [local(): stats = lax.all_to_all(stats, 'kcol', 0, 0, tiled=True)]
    dot_general x2 -> x0, matrix products: 11.9 us -> none  [the longest x1 11.4 us: local(): jnp.einsum('snf,sfd->nd', hidden, down_all, preferred_element_type=jnp.fl...]
  transfers between devices with their start and end apart: 5 -> 30, of which waited for: 3 -> 4; matrix products, arithmetic and copies ran while one was open for 12% -> 23% of each run, Pallas kernels for 24% -> 24%
where the time goes in v2:
time: 250 us; the launch traced here: 245 us
  Pallas kernels  73.7 us (29%)
  starting transfers between devices  61 us (24%)
  local copies, waits for them, and re-layouts  41.4 us (17%)
  waiting for transfers between devices  29.3 us (12%)
  matrix products  20.7 us (8%)
  between operations  13.7 us (5%)
  other arithmetic  5.41 us (2%)
    pallas_call x4, Pallas kernels, edge_stage(): pl.pallas_call(functools.partial(edge_kernel, start), grid_spec=grid_spec...  29.9 us
    ppermute x4, starting transfers between devices, swap_core(): return lax.ppermute(value, 'kcol', [(i, i ^ 1) for i in range(8)])  28 us
    unnamed x59, local copies, waits for them, and re-layouts  25.3 us
    pallas_call x1, Pallas kernels, attend_stage(): pl.pallas_call(attend_kernel, grid_spec=grid_spec, out_shape=[jax.ShapeDt...  22.5 us
    ppermute x9, waiting for transfers between devices, shift_chip(): return lax.ppermute(value, 'kcol', [(i, i + 2 * by & 7) for i in range(8)])  16.8 us
    pallas_call x1, Pallas kernels, tail_stage(): pl.pallas_call(tail_kernel, grid_spec=grid_spec, out_shape=jax.ShapeDtype...  15.1 us
    ppermute x8, starting transfers between devices, shift_high(): lax.ppermute(value, 'qrow', [(i, i + 4 * by & 15) for i in range(16)])  12.6 us
    ppermute x4, waiting for transfers between devices, swap_core(): return lax.ppermute(value, 'kcol', [(i, i ^ 1) for i in range(8)])  12.4 us
  transfers between devices with their start and end apart: 30, of which 4 were waited for; matrix products, arithmetic and copies ran while one was open for 23% of the time, Pallas kernels for 24%

profile of v2, /device:TPU:1, one launch (start us, length us, event | category | flops | bytes accessed | tf_op | source)
XLA Modules:
  0.0 245.1 jit_solution(907781079515058243)
XLA Ops:
  12.6 2.5 %collective-permute-start.6 = (bf16[64,1024]{1,0:T(8,128)(2,1)}, bf16[64,1024]{1,0:T(8,128)(2,1)}, u32[]{:S(2)}, u32[]{:S(2)}) collective-permute-start(bf16[64,1024]{1,0:T(8,128)(2,1)} %get-tuple-element.60), channel_id=1, source_target_pairs={{0,32},{8,40},{16,48},{24,56},{32,64},{40,72},{48,80},{56,88},{64,... | collective-permute-start | bytes 393224 | tf_op jit(solution)/shard_map/ppermute | solution.py:426
  28.7 10.2 %edge_terms.4 = (bf16[32,16,128,128]{3,2,1,0:T(8,128)(2,1)}, bf16[32,16,128,128]{3,2,1,0:T(8,128)(2,1)}) custom-call(s32[8,32]{1,0:T(8,128)} %lists.1, f32[32]{0:T(128)} %get-tuple-element.47.offsets, bf16[32,128,128]{2,1,0:T(8,128)(2,1)} %bitcast.37, bf16[256,512]{1,0:T(8,128)(2,1)} %mul.58.mix_ref, f32[64,128]{1,0:T(8,128)} %broadcast_in_dim.14.scale_ref, ...), custom_call_target="tpu_custom_call" | custom-call | flops 6442450944 | bytes 6291456 | tf_op jit(solution)/shard_map/edge_terms/pallas_call | solution.py:134
  52.5 2.5 %collective-permute-start.13 = (bf16[128,1024]{1,0:T(8,128)(2,1)S(1)}, bf16[128,1024]{1,0:T(8,128)(2,1)S(1)}, u32[]{:S(2)}, u32[]{:S(2)}) collective-permute-start(bf16[128,1024]{1,0:T(8,128)(2,1)S(1)} %get-tuple-element.26), channel_id=1, source_target_pairs={{0,6},{1,7},{2,0},{3,1},{4,2},{5,3},{6,4},{7,5},{8,14},{9,15},{10,... | collective-permute-start | bytes 786440 | tf_op jit(solution)/shard_map/ppermute | solution.py:430
  56.2 2.7 %collective-permute-start.11 = (bf16[256,1024]{1,0:T(8,128)(2,1)}, bf16[256,1024]{1,0:T(8,128)(2,1)S(1)}, u32[]{:S(2)}, u32[]{:S(2)}) collective-permute-start(bf16[256,1024]{1,0:T(8,128)(2,1)} %get-tuple-element.78), channel_id=1, source_target_pairs={{0,24},{8,0},{16,8},{24,16},{32,56},{40,32},{48,40},{56,48},{64,88... | collective-permute-start | bytes 1572872 | tf_op jit(solution)/shard_map/ppermute | solution.py:422
  60.2 2.7 %collective-permute-start.5 = (bf16[256,1024]{1,0:T(8,128)(2,1)}, bf16[256,1024]{1,0:T(8,128)(2,1)S(1)}, u32[]{:S(2)}, u32[]{:S(2)}) collective-permute-start(bf16[256,1024]{1,0:T(8,128)(2,1)} %get-tuple-element.74), channel_id=1, source_target_pairs={{0,96},{8,104},{16,112},{24,120},{32,0},{40,8},{48,16},{56,24},{64... | collective-permute-start | bytes 1572872 | tf_op jit(solution)/shard_map/ppermute | solution.py:426
  62.9 9.3 %edge_terms.5 = (bf16[32,16,128,128]{3,2,1,0:T(8,128)(2,1)}, bf16[32,16,128,128]{3,2,1,0:T(8,128)(2,1)}) custom-call(s32[8,32]{1,0:T(8,128)} %lists.1, f32[32]{0:T(128)} %get-tuple-element.47.offsets, bf16[32,128,128]{2,1,0:T(8,128)(2,1)} %bitcast.38, bf16[256,512]{1,0:T(8,128)(2,1)} %mul.58.mix_ref, ...), custom_call_target="tpu_custom_call", output_to_operand_aliasing={{0}: (6, {}), {1}: (7, {})} | custom-call | flops 5368709120 | bytes 5242880 | tf_op jit(solution)/shard_map/edge_terms/pallas_call | solution.py:134
  75.8 7.5 %edge_terms.6 = (bf16[32,16,128,128]{3,2,1,0:T(8,128)(2,1)}, bf16[32,16,128,128]{3,2,1,0:T(8,128)(2,1)}) custom-call(s32[8,32]{1,0:T(8,128)} %lists.1, f32[32]{0:T(128)} %get-tuple-element.47.offsets, bf16[32,128,128]{2,1,0:T(8,128)(2,1)} %bitcast.39, bf16[256,512]{1,0:T(8,128)(2,1)} %mul.58.mix_ref, ...), custom_call_target="tpu_custom_call", output_to_operand_aliasing={{0}: (6, {}), {1}: (7, {})} | custom-call | flops 11811160064 | bytes 11534336 | tf_op jit(solution)/shard_map/edge_terms/pallas_call | solution.py:134
  86.0 15.3 %collective-permute-start.19 = (bf16[512,1024]{1,0:T(8,128)(2,1)}, bf16[512,1024]{1,0:T(8,128)(2,1)S(1)}, u32[]{:S(2)}, u32[]{:S(2)}) collective-permute-start(bf16[512,1024]{1,0:T(8,128)(2,1)} %pad_maximum_fusion.7), channel_id=1, source_target_pairs={{0,1},{1,0},{2,3},{3,2},{4,5},{5,4},{6,7},{7,6},{8,9},{9,8},{10,11... | collective-permute-start | bytes 3145736 | tf_op jit(solution)/shard_map/ppermute | solution.py:438
  103.5 2.7 %collective-permute-start.18 = (bf16[128,1024]{1,0:T(8,128)(2,1)}, bf16[128,1024]{1,0:T(8,128)(2,1)}, u32[]{:S(2)}, u32[]{:S(2)}) collective-permute-start(bf16[128,1024]{1,0:T(8,128)(2,1)} %slice.97), channel_id=1, source_target_pairs={{0,24},{8,0},{16,8},{24,16},{32,56},{40,32},{48,40},{56,48},{64,88... | collective-permute-start | bytes 786440 | tf_op jit(solution)/shard_map/ppermute | solution.py:422
  107.6 2.7 %collective-permute-start.16 = (bf16[128,1024]{1,0:T(8,128)(2,1)}, bf16[128,1024]{1,0:T(8,128)(2,1)}, u32[]{:S(2)}, u32[]{:S(2)}) collective-permute-start(bf16[128,1024]{1,0:T(8,128)(2,1)} %slice.95), channel_id=1, source_target_pairs={{0,96},{8,104},{16,112},{24,120},{32,0},{40,8},{48,16},{56,24},{64... | collective-permute-start | bytes 786440 | tf_op jit(solution)/shard_map/ppermute | solution.py:426
  110.3 2.9 %edge_terms.7 = (bf16[32,16,128,128]{3,2,1,0:T(8,128)(2,1)}, bf16[32,16,128,128]{3,2,1,0:T(8,128)(2,1)}) custom-call(s32[8,32]{1,0:T(8,128)} %lists.1, f32[32]{0:T(128)} %get-tuple-element.47.offsets, bf16[32,128,128]{2,1,0:T(8,128)(2,1)} %bitcast.40, bf16[256,512]{1,0:T(8,128)(2,1)} %mul.58.mix_ref, ...), custom_call_target="tpu_custom_call", output_to_operand_aliasing={{0}: (6, {}), {1}: (7, {})} | custom-call | flops 10737418240 | bytes 10485760 | tf_op jit(solution)/shard_map/edge_terms/pallas_call | solution.py:134
  119.6 7.5 %convert_bitcast_fusion.value_ref = bf16[16,1024,128]{2,1,0:T(8,128)(2,1)} fusion(bf16[16,64,1024]{2,1,0:T(8,128)(2,1)S(1)} %bitcast.43, bf16[16,64,1024]{2,1,0:T(8,128)(2,1)} %bitcast.8, bf16[1024,1024]{1,0:T(8,128)(2,1)S(1)} %copy-done), kind=kOutput, calls=%fused_computation.1 | convolution fusion | flops 4305453056 | bytes 10485760 | tf_op jit(solution)/shard_map/kd,gnk->gdn/dot_general | solution.py:539
  127.1 7.9 %fusion.2.key_ref = bf16[16,128,1024]{2,1,0:T(8,128)(2,1)} fusion(bf16[16,64,1024]{2,1,0:T(8,128)(2,1)S(1)} %bitcast.44, bf16[16,64,1024]{2,1,0:T(8,128)(2,1)} %bitcast.8, bf16[1024,1024]{1,0:T(8,128)(2,1)S(1)} %copy-done.16), kind=kOutput, calls=%fused_computation.4 | convolution fusion | flops 4305453056 | bytes 10485760 | tf_op jit(solution)/shard_map/gnk,kd->gnd/dot_general | solution.py:536
  136.6 3.6 %multiply_bitcast_fusion.query_ref = bf16[8,1024,128]{2,1,0:T(8,128)(2,1)} fusion(bf16[8,128,1024]{2,1,0:T(8,128)(2,1)S(1)} %bitcast.45, bf16[1024,1024]{1,0:T(8,128)(2,1)S(1)} %copy-done.17), kind=kOutput, calls=%fused_computation.9 | convolution fusion | flops 2149580800 | bytes 6291456 | tf_op jit(solution)/shard_map/kd,gnk->gdn/dot_general | solution.py:531
  140.2 22.5 %attend.1 = (bf16[8,1024,128]{2,1,0:T(8,128)(2,1)}, f32[8,32,128]{2,1,0:T(8,128)}) custom-call(s32[8,32]{1,0:T(8,128)} %lists.1, f32[16]{0:T(128)} %slopes.1, f32[32]{0:T(128)} %get-tuple-element.47.offsets, bf16[32,128,128]{2,1,0:T(8,128)(2,1)} %bitcast.41, bf16[32,16,128,128]{3,2,1,0:T(8,128)(2,1)} %get-tuple-element.37.bias_ref, ...), custom_call_target="tpu_custom_call" | custom-call | flops 8589934592 | bytes 33554432 | tf_op jit(solution)/shard_map/attend/pallas_call | solution.py:253
  162.7 12.0 %collective-permute-start.28 = (bf16[16,1024,256]{2,1,0:T(8,128)(2,1)}, bf16[16,1024,256]{2,1,0:T(8,128)(2,1)}, u32[]{:S(2)}, u32[]{:S(2)}) collective-permute-start(bf16[16,1024,256]{2,1,0:T(8,128)(2,1)} %bitcast.35), channel_id=1, source_target_pairs={{0,1},{1,0},{2,3},{3,2},{4,5},{5,4},{6,7},{7,6},{8,9},{9,8},{10,11... | collective-permute-start | bytes 25165832 | tf_op jit(solution)/shard_map/ppermute | solution.py:438
  176.7 12.4 %collective-permute-done.21.other_stat = f32[4,32,128]{2,1,0:T(8,128)S(1)} collective-permute-done((f32[4,32,128]{2,1,0:T(8,128)S(1)}, f32[4,32,128]{2,1,0:T(8,128)S(1)}, u32[]{:S(2)}, u32[]{:S(2)}) %collective-permute-start.21) | collective-permute-done | bytes 65568 | tf_op jit(solution)/shard_map/ppermute | solution.py:438
  190.7 3.8 %merge.1 = (bf16[4,1024,128]{2,1,0:T(8,128)(2,1)}, f32[4,32,128]{2,1,0:T(8,128)}) custom-call(bf16[8,1024,128]{2,1,0:T(8,128)(2,1)} %get-tuple-element.40.own_ref, bf16[4,1024,128]{2,1,0:T(8,128)(2,1)} %copy-done.7, f32[8,32,128]{2,1,0:T(8,128)} %get-tuple-element.41.own_stat, f32[4,32,128]{2,1,0:T(8,128)} %copy-done.10), custom_call_target="tpu_custom_call" | custom-call | tf_op jit(solution)/shard_map/merge/pallas_call | solution.py:300
  198.1 2.4 collective-permute-start.25
  200.5 8.9 %collective-permute-done.25.stat_1 = f32[1,32,128]{2,1,0:T(8,128)S(1)} collective-permute-done((f32[1,32,128]{2,1,0:T(8,128)S(1)}, f32[1,32,128]{2,1,0:T(8,128)S(1)}, u32[]{:S(2)}, u32[]{:S(2)}) %collective-permute-start.25) | collective-permute-done | bytes 16416 | tf_op jit(solution)/shard_map/ppermute | solution.py:430
  209.4 3.8 %collective-permute-done.26.stat_2 = f32[1,32,128]{2,1,0:T(8,128)S(1)} collective-permute-done((f32[1,32,128]{2,1,0:T(8,128)S(1)}, f32[1,32,128]{2,1,0:T(8,128)S(1)}, u32[]{:S(2)}, u32[]{:S(2)}) %collective-permute-start.26) | collective-permute-done | bytes 16416 | tf_op jit(solution)/shard_map/ppermute | solution.py:430
  213.2 4.1 %collective-permute-done.27.stat_3 = f32[1,32,128]{2,1,0:T(8,128)S(1)} collective-permute-done((f32[1,32,128]{2,1,0:T(8,128)S(1)}, f32[1,32,128]{2,1,0:T(8,128)S(1)}, u32[]{:S(2)}, u32[]{:S(2)}) %collective-permute-start.27) | collective-permute-done | bytes 16416 | tf_op jit(solution)/shard_map/ppermute | solution.py:430
  217.3 3.4 %copy-done.2 = bf16[16384,256]{1,0:T(8,128)(2,1)S(1)} copy-done((bf16[16384,256]{1,0:T(8,128)(2,1)S(1)}, bf16[16384,256]{1,0:T(8,128)(2,1)}, u32[]{:S(2)}) %copy-start.2) | copy-done | bytes 8388632
  223.1 15.1 %tail.1 = bf16[128,1024]{1,0:T(8,128)(2,1)} custom-call(s32[1]{0:T(128)} %bitcast.core, bf16[4,1024,128]{2,1,0:T(8,128)(2,1)S(1)} %copy-done.3, bf16[1,1024,128]{2,1,0:T(8,128)(2,1)S(1)} %collective-permute-done.22.part_1, bf16[1,1024,128]{2,1,0:T(8,128)(2,1)S(1)} %collective-permute-done.23.part_2, ...), custom_call_target="tpu_custom_call" | custom-call | flops 2147483648 | bytes 16777216 | tf_op jit(solution)/shard_map/tail/pallas_call | solution.py:397
  (142 shorter events, 63.1 us)
Async XLA Ops:
  6.5 156.2 %all-gather.3.cloned.1.call-start = ((), (), s32[]{:S(2)}) async-start(), calls=%async_computation | async-start | bytes 8912896 | tf_op jit(solution)/shard_map/all_gather | solution.py:472
  12.6 26.3 %collective-permute-start.6 = (bf16[64,1024]{1,0:T(8,128)(2,1)}, bf16[64,1024]{1,0:T(8,128)(2,1)}, u32[]{:S(2)}, u32[]{:S(2)}) collective-permute-start(bf16[64,1024]{1,0:T(8,128)(2,1)} %get-tuple-element.60), channel_id=1, source_target_pairs={{0,32},{8,40},{16,48},{24,56},{32,64},{40,72},{48,80},{56,88},{64,... | collective-permute-start | bytes 393224 | tf_op jit(solution)/shard_map/ppermute | solution.py:426
  15.0 25.3 %collective-permute-start.7 = (bf16[64,1024]{1,0:T(8,128)(2,1)}, bf16[64,1024]{1,0:T(8,128)(2,1)}, u32[]{:S(2)}, u32[]{:S(2)}) collective-permute-start(bf16[64,1024]{1,0:T(8,128)(2,1)} %get-tuple-element.60), channel_id=1, source_target_pairs={{0,96},{8,104},{16,112},{24,120},{32,0},{40,8},{48,16},{56,24},{64... | collective-permute-start | bytes 393224 | tf_op jit(solution)/shard_map/ppermute | solution.py:426
  17.1 26.1 %collective-permute-start = (bf16[64,1024]{1,0:T(8,128)(2,1)}, bf16[64,1024]{1,0:T(8,128)(2,1)}, u32[]{:S(2)}, u32[]{:S(2)}) collective-permute-start(bf16[64,1024]{1,0:T(8,128)(2,1)} %get-tuple-element.61), channel_id=1, source_target_pairs={{0,8},{8,16},{16,24},{24,0},{32,40},{40,48},{48,56},{56,32},{64,72... | collective-permute-start | bytes 393224 | tf_op jit(solution)/shard_map/ppermute | solution.py:422
  18.4 26.7 %collective-permute-start.1 = (bf16[64,1024]{1,0:T(8,128)(2,1)}, bf16[64,1024]{1,0:T(8,128)(2,1)S(1)}, u32[]{:S(2)}, u32[]{:S(2)}) collective-permute-start(bf16[64,1024]{1,0:T(8,128)(2,1)} %get-tuple-element.61), channel_id=1, source_target_pairs={{0,24},{8,0},{16,8},{24,16},{32,56},{40,32},{48,40},{56,48},{64,88... | collective-permute-start | bytes 393224 | tf_op jit(solution)/shard_map/ppermute | solution.py:422
  19.9 40.3 %collective-permute-start.12 = (bf16[128,1024]{1,0:T(8,128)(2,1)S(1)}, bf16[128,1024]{1,0:T(8,128)(2,1)}, u32[]{:S(2)}, u32[]{:S(2)}) collective-permute-start(bf16[128,1024]{1,0:T(8,128)(2,1)S(1)} %get-tuple-element.26), channel_id=1, source_target_pairs={{0,2},{1,3},{2,4},{3,5},{4,6},{5,7},{6,0},{7,1},{8,10},{9,11},{10,... | collective-permute-start | bytes 786440 | tf_op jit(solution)/shard_map/ppermute | solution.py:430
  39.7 12.7 %collective-permute-start.8 = (bf16[32,1024]{1,0:T(8,128)(2,1)S(1)}, bf16[32,1024]{1,0:T(8,128)(2,1)S(1)}, u32[]{:S(2)}, u32[]{:S(2)}) collective-permute-start(bf16[32,1024]{1,0:T(8,128)(2,1)S(1)} %slice.92), channel_id=1, source_target_pairs={{0,32},{8,40},{16,48},{24,56},{32,64},{40,72},{48,80},{56,88},{64,... | collective-permute-start | bytes 196616 | tf_op jit(solution)/shard_map/ppermute | solution.py:426
  41.1 14.4 %collective-permute-start.9 = (bf16[32,1024]{1,0:T(8,128)(2,1)S(1)}, bf16[32,1024]{1,0:T(8,128)(2,1)S(1)}, u32[]{:S(2)}, u32[]{:S(2)}) collective-permute-start(bf16[32,1024]{1,0:T(8,128)(2,1)S(1)} %slice.93), channel_id=1, source_target_pairs={{0,96},{8,104},{16,112},{24,120},{32,0},{40,8},{48,16},{56,24},{64... | collective-permute-start | bytes 196616 | tf_op jit(solution)/shard_map/ppermute | solution.py:426
  44.1 12.1 %collective-permute-start.2 = (bf16[32,1024]{1,0:T(8,128)(2,1)S(1)}, bf16[32,1024]{1,0:T(8,128)(2,1)S(1)}, u32[]{:S(2)}, u32[]{:S(2)}) collective-permute-start(bf16[32,1024]{1,0:T(8,128)(2,1)S(1)} %slice.89), channel_id=1, source_target_pairs={{0,8},{8,16},{16,24},{24,0},{32,40},{40,48},{48,56},{56,32},{64,72... | collective-permute-start | bytes 196616 | tf_op jit(solution)/shard_map/ppermute | solution.py:422
  45.2 14.4 %collective-permute-start.3 = (bf16[32,1024]{1,0:T(8,128)(2,1)S(1)}, bf16[32,1024]{1,0:T(8,128)(2,1)S(1)}, u32[]{:S(2)}, u32[]{:S(2)}) collective-permute-start(bf16[32,1024]{1,0:T(8,128)(2,1)S(1)} %slice.90), channel_id=1, source_target_pairs={{0,24},{8,0},{16,8},{24,16},{32,56},{40,32},{48,40},{56,48},{64,88... | collective-permute-start | bytes 196616 | tf_op jit(solution)/shard_map/ppermute | solution.py:422
  52.5 21.4 %collective-permute-start.13 = (bf16[128,1024]{1,0:T(8,128)(2,1)S(1)}, bf16[128,1024]{1,0:T(8,128)(2,1)S(1)}, u32[]{:S(2)}, u32[]{:S(2)}) collective-permute-start(bf16[128,1024]{1,0:T(8,128)(2,1)S(1)} %get-tuple-element.26), channel_id=1, source_target_pairs={{0,6},{1,7},{2,0},{3,1},{4,2},{5,3},{6,4},{7,5},{8,14},{9,15},{10,... | collective-permute-start | bytes 786440 | tf_op jit(solution)/shard_map/ppermute | solution.py:430
  56.2 45.8 %collective-permute-start.10 = (bf16[256,1024]{1,0:T(8,128)(2,1)}, bf16[256,1024]{1,0:T(8,128)(2,1)S(1)}, u32[]{:S(2)}, u32[]{:S(2)}) collective-permute-start(bf16[256,1024]{1,0:T(8,128)(2,1)} %get-tuple-element.78), channel_id=1, source_target_pairs={{0,8},{8,16},{16,24},{24,0},{32,40},{40,48},{48,56},{56,32},{64,72... | collective-permute-start | bytes 1572872 | tf_op jit(solution)/shard_map/ppermute | solution.py:422
  56.2 46.5 %collective-permute-start.11 = (bf16[256,1024]{1,0:T(8,128)(2,1)}, bf16[256,1024]{1,0:T(8,128)(2,1)S(1)}, u32[]{:S(2)}, u32[]{:S(2)}) collective-permute-start(bf16[256,1024]{1,0:T(8,128)(2,1)} %get-tuple-element.78), channel_id=1, source_target_pairs={{0,24},{8,0},{16,8},{24,16},{32,56},{40,32},{48,40},{56,48},{64,88... | collective-permute-start | bytes 1572872 | tf_op jit(solution)/shard_map/ppermute | solution.py:422
  60.2 45.9 %collective-permute-start.4 = (bf16[256,1024]{1,0:T(8,128)(2,1)}, bf16[256,1024]{1,0:T(8,128)(2,1)S(1)}, u32[]{:S(2)}, u32[]{:S(2)}) collective-permute-start(bf16[256,1024]{1,0:T(8,128)(2,1)} %get-tuple-element.74), channel_id=1, source_target_pairs={{0,32},{8,40},{16,48},{24,56},{32,64},{40,72},{48,80},{56,88},{64,... | collective-permute-start | bytes 1572872 | tf_op jit(solution)/shard_map/ppermute | solution.py:426
  60.2 46.7 %collective-permute-start.5 = (bf16[256,1024]{1,0:T(8,128)(2,1)}, bf16[256,1024]{1,0:T(8,128)(2,1)S(1)}, u32[]{:S(2)}, u32[]{:S(2)}) collective-permute-start(bf16[256,1024]{1,0:T(8,128)(2,1)} %get-tuple-element.74), channel_id=1, source_target_pairs={{0,96},{8,104},{16,112},{24,120},{32,0},{40,8},{48,16},{56,24},{64... | collective-permute-start | bytes 1572872 | tf_op jit(solution)/shard_map/ppermute | solution.py:426
  86.0 49.1 %collective-permute-start.19 = (bf16[512,1024]{1,0:T(8,128)(2,1)}, bf16[512,1024]{1,0:T(8,128)(2,1)S(1)}, u32[]{:S(2)}, u32[]{:S(2)}) collective-permute-start(bf16[512,1024]{1,0:T(8,128)(2,1)} %pad_maximum_fusion.7), channel_id=1, source_target_pairs={{0,1},{1,0},{2,3},{3,2},{4,5},{5,4},{6,7},{7,6},{8,9},{9,8},{10,11... | collective-permute-start | bytes 3145736 | tf_op jit(solution)/shard_map/ppermute | solution.py:438
  102.8 12.2 %collective-permute-start.17 = (bf16[128,1024]{1,0:T(8,128)(2,1)}, bf16[128,1024]{1,0:T(8,128)(2,1)S(1)}, u32[]{:S(2)}, u32[]{:S(2)}) collective-permute-start(bf16[128,1024]{1,0:T(8,128)(2,1)} %slice.96), channel_id=1, source_target_pairs={{0,8},{8,16},{16,24},{24,0},{32,40},{40,48},{48,56},{56,32},{64,72... | collective-permute-start | bytes 786440 | tf_op jit(solution)/shard_map/ppermute | solution.py:422
  103.5 11.5 %collective-permute-start.18 = (bf16[128,1024]{1,0:T(8,128)(2,1)}, bf16[128,1024]{1,0:T(8,128)(2,1)}, u32[]{:S(2)}, u32[]{:S(2)}) collective-permute-start(bf16[128,1024]{1,0:T(8,128)(2,1)} %slice.97), channel_id=1, source_target_pairs={{0,24},{8,0},{16,8},{24,16},{32,56},{40,32},{48,40},{56,48},{64,88... | collective-permute-start | bytes 786440 | tf_op jit(solution)/shard_map/ppermute | solution.py:422
  162.7 54.5 %collective-permute-start.28 = (bf16[16,1024,256]{2,1,0:T(8,128)(2,1)}, bf16[16,1024,256]{2,1,0:T(8,128)(2,1)}, u32[]{:S(2)}, u32[]{:S(2)}) collective-permute-start(bf16[16,1024,256]{2,1,0:T(8,128)(2,1)} %bitcast.35), channel_id=1, source_target_pairs={{0,1},{1,0},{2,3},{3,2},{4,5},{5,4},{6,7},{7,6},{8,9},{9,8},{10,11... | collective-permute-start | bytes 25165832 | tf_op jit(solution)/shard_map/ppermute | solution.py:438
  176.0 13.1 %collective-permute-start.20 = (bf16[4,1024,128]{2,1,0:T(8,128)(2,1)S(1)}, bf16[4,1024,128]{2,1,0:T(8,128)(2,1)S(1)}, u32[]{:S(2)}, u32[]{:S(2)}) collective-permute-start(bf16[4,1024,128]{2,1,0:T(8,128)(2,1)S(1)} %slice.80), channel_id=1, source_target_pairs={{0,1},{1,0},{2,3},{3,2},{4,5},{5,4},{6,7},{7,6},{8,9},{9,8},{10,11... | collective-permute-start | bytes 3145736 | tf_op jit(solution)/shard_map/ppermute | solution.py:438
  176.1 13.0 %collective-permute-start.21 = (f32[4,32,128]{2,1,0:T(8,128)S(1)}, f32[4,32,128]{2,1,0:T(8,128)S(1)}, u32[]{:S(2)}, u32[]{:S(2)}) collective-permute-start(f32[4,32,128]{2,1,0:T(8,128)S(1)} %slice.81), channel_id=1, source_target_pairs={{0,1},{1,0},{2,3},{3,2},{4,5},{5,4},{6,7},{7,6},{8,9},{9,8},{10,11... | collective-permute-start | bytes 196616 | tf_op jit(solution)/shard_map/ppermute | solution.py:438
  195.8 21.5 %collective-permute-start.22 = (bf16[1,1024,128]{2,1,0:T(8,128)(2,1)S(1)}, bf16[1,1024,128]{2,1,0:T(8,128)(2,1)S(1)}, u32[]{:S(2)}, u32[]{:S(2)}) collective-permute-start(bf16[1,1024,128]{2,1,0:T(8,128)(2,1)S(1)} %get-tuple-element.51), channel_id=1, source_target_pairs={{0,6},{1,7},{2,0},{3,1},{4,2},{5,3},{6,4},{7,5},{8,14},{9,15},{10,... | collective-permute-start | bytes 786440 | tf_op jit(solution)/shard_map/ppermute | solution.py:430
  195.9 21.4 %collective-permute-start.23 = (bf16[1,1024,128]{2,1,0:T(8,128)(2,1)S(1)}, bf16[1,1024,128]{2,1,0:T(8,128)(2,1)S(1)}, u32[]{:S(2)}, u32[]{:S(2)}) collective-permute-start(bf16[1,1024,128]{2,1,0:T(8,128)(2,1)S(1)} %get-tuple-element.50), channel_id=1, source_target_pairs={{0,2},{1,3},{2,4},{3,5},{4,6},{5,7},{6,0},{7,1},{8,10},{9,11},{10,... | collective-permute-start | bytes 786440 | tf_op jit(solution)/shard_map/ppermute | solution.py:430
  197.3 19.9 %collective-permute-start.24 = (bf16[1,1024,128]{2,1,0:T(8,128)(2,1)S(1)}, bf16[1,1024,128]{2,1,0:T(8,128)(2,1)S(1)}, u32[]{:S(2)}, u32[]{:S(2)}) collective-permute-start(bf16[1,1024,128]{2,1,0:T(8,128)(2,1)S(1)} %get-tuple-element.49), channel_id=1, source_target_pairs={{0,4},{1,5},{2,6},{3,7},{4,0},{5,1},{6,2},{7,3},{8,12},{9,13},{10,... | collective-permute-start | bytes 786440 | tf_op jit(solution)/shard_map/ppermute | solution.py:430
  (26 other events, 335.6 us)
Sparse Core Ops, SparseCore 0:
  9.5 86.2 all-gather.2
